TPU v7x, 512 devices: a whole 4x8x8 slice. The times are simulated.
512 devices in a mesh: rows: 16 (over y, z_hi), cols: 32 (over x, z_lo, core).
Axes of the slice: x: 4, y: 8, z: 8 (z_hi: 2, z_lo: 4; z = z_hi * 4 + z_lo), core: 2. Of those that a mesh axis runs over, the one named last changes fastest.
Arguments:
- pair: bfloat16 [1024, 1024, 128], P('rows', 'cols'), may hold values from -6 to 6
- length: int32 [1], replicated, may hold values from 256 to 1024
- ln_gain: float32 [128], replicated, may hold values from 0.25 to 1.75
- w_query: bfloat16 [128, 128], replicated, may hold values from -8 to 8
- w_key: bfloat16 [128, 128], replicated, may hold values from -8 to 8
- w_value: bfloat16 [128, 128], replicated, may hold values from -0.5 to 0.5
- w_gate: bfloat16 [128, 128], replicated, may hold values from -0.5 to 0.5
- w_bias: bfloat16 [128, 4], replicated, may hold values from -0.5 to 0.5
- w_out: bfloat16 [128, 128], replicated, may hold values from -0.5 to 0.5
- out_grad: bfloat16 [128, 1024, 128], P('rows', 'cols'), may hold values from -6 to 6
Outputs:
- update: bfloat16 [128, 1024, 128], P('rows', 'cols')
- pair_grad: float32 [1024, 1024, 128], P('rows', 'cols')
Inputs may be any that keep to these rules, and one draw needn't show every extreme that they name: Keys at positions (length) and beyond are padding.
All inputs are finite; a program needn't handle non-finite values.
Results may differ from a plain program's by a relative error of at most 0.03.
The roundings to bfloat16 on the way count: a program that leaves them out, or rounds other values in their place, can miss the bound.
Values may be sent and summed in bfloat16 or wider, within the bound.
A program may use at most 64 MiB of HBM per device.

v0:
```python
import jax
import jax.numpy as jnp
from jax import lax
from jax.sharding import PartitionSpec as P

EPS = 1e-05
NEG = -1000000000.0


def broadcast(value, axis, source):
    kept = jnp.where(lax.axis_index(axis) == source, value, 0).astype(value.dtype)
    return lax.psum(kept, axis)


def layer_norm(values, gain_vec):
    average = jnp.mean(values, axis=-1, keepdims=True)
    centred = values - average
    variance = jnp.mean(centred * centred, axis=-1, keepdims=True)
    return centred * lax.rsqrt(variance + EPS) * gain_vec


def body(pair, length, ln_gain, w_query, w_key, w_value, w_gate, w_bias, w_out, out_grad):
    rows_blk, cols_blk, channels = pair.shape
    window_rows = out_grad.shape[0]
    head_count = w_bias.shape[1]
    head_dim = channels // head_count
    score_scale = head_dim ** (-0.5)
    col_index = lax.axis_index("cols")
    f32 = jnp.float32
    bf16 = jnp.bfloat16

    def split_heads(values):
        return values.reshape(values.shape[0], values.shape[1], head_count, head_dim)

    def key_mask(offset, extent):
        return offset + jnp.arange(extent) < length[0]

    def scores(query_heads, key_heads, bias_part, keep):
        logits = jnp.einsum("ijhd,ikhd->ihjk", query_heads, key_heads, preferred_element_type=f32)
        logits = logits + bias_part.astype(f32)[None]
        return jnp.where(keep, logits, NEG)

    pair_f = pair.astype(f32)
    normed = layer_norm(pair_f, ln_gain).astype(bf16)
    bias_tile = jnp.einsum("ijc,ch->hij", normed, w_bias, preferred_element_type=f32).astype(bf16)
    bias_cols = lax.all_gather(bias_tile, "rows", axis=1, tiled=True)
    bias_band = lax.all_gather(bias_tile, "cols", axis=2, tiled=True)
    source_row = col_index * cols_blk // rows_blk
    bias_band = broadcast(bias_band, "rows", source_row)
    band_offset = col_index * cols_blk % rows_blk
    bias_rows = lax.dynamic_slice_in_dim(bias_band, band_offset, cols_blk, 1)
    window = normed[:window_rows]
    query = (jnp.dot(window, w_query, preferred_element_type=f32) * score_scale).astype(bf16)
    key_proj = jnp.dot(window, w_key, preferred_element_type=f32).astype(bf16)
    value_proj = jnp.dot(window, w_value, preferred_element_type=f32).astype(bf16)
    gate = jax.nn.sigmoid(jnp.dot(window, w_gate, preferred_element_type=f32)).astype(bf16)
    query_heads = split_heads(query)
    maxima = jnp.full((window_rows, head_count, cols_blk), -jnp.inf, f32)
    totals = jnp.zeros((window_rows, head_count, cols_blk), f32)
    summed = jnp.zeros((window_rows, head_count, cols_blk, head_dim), f32)
    key_piece = lax.all_gather(key_proj, "cols", axis=1, tiled=True)
    value_piece = lax.all_gather(value_proj, "cols", axis=1, tiled=True)
    extent = key_piece.shape[1]
    bias_part = bias_rows
    logits = scores(query_heads, split_heads(key_piece), bias_part, key_mask(jnp.int32(0), extent))
    new_max = logits.max(-1)
    shrink = jnp.exp(maxima - new_max)
    expo = jnp.exp(logits - new_max[..., None])
    totals = totals * shrink + expo.sum(-1)
    summed = summed * shrink[..., None] + jnp.einsum(
        "ihjk,ikhd->ihjd", expo.astype(bf16), split_heads(value_piece), preferred_element_type=f32
    )
    maxima, totals, summed = (new_max, totals, summed)
    lse = maxima + jnp.log(totals)
    attended = (
        (summed / totals[..., None]).transpose(0, 2, 1, 3).reshape(window_rows, cols_blk, channels)
    )
    gate_f = gate.astype(f32)
    gated = (gate_f * attended).astype(bf16)
    update = jnp.dot(gated, w_out, preferred_element_type=f32).astype(bf16)
    grad_gated = lax.dot_general(
        out_grad, w_out, (((2,), (1,)), ((), ())), preferred_element_type=f32
    )
    grad_attn = (grad_gated * gate_f).astype(bf16)
    grad_pre = grad_gated * attended * gate_f * (1.0 - gate_f)
    delta = jnp.sum(split_heads(grad_attn).astype(f32) * split_heads(attended), -1)
    delta_heads = delta.transpose(0, 2, 1)
    grad_heads = split_heads(grad_attn)
    key_piece = lax.all_gather(key_proj, "cols", axis=1, tiled=True)
    value_piece = lax.all_gather(value_proj, "cols", axis=1, tiled=True)
    extent = key_piece.shape[1]
    bias_part = bias_rows
    key_heads = split_heads(key_piece)
    logits = scores(query_heads, key_heads, bias_part, key_mask(jnp.int32(0), extent))
    shares = jnp.exp(logits - lse[..., None])
    grad_shares = jnp.einsum(
        "ijhd,ikhd->ihjk", grad_heads, split_heads(value_piece), preferred_element_type=f32
    )
    grad_logits = (shares * (grad_shares - delta_heads[..., None])).astype(bf16)
    grad_query = jnp.einsum("ihjk,ikhd->ijhd", grad_logits, key_heads, preferred_element_type=f32)
    lse_all, delta_all = (
        lax.all_gather(lse.transpose(0, 2, 1), "cols", axis=1, tiled=True),
        lax.all_gather(delta, "cols", axis=1, tiled=True),
    )
    key_heads_own = split_heads(key_proj)
    value_heads_own = split_heads(value_proj)
    own_keep = key_mask(col_index * cols_blk, cols_blk)
    query_piece = lax.all_gather(query, "cols", axis=1, tiled=True)
    grad_piece = lax.all_gather(grad_attn, "cols", axis=1, tiled=True)
    extent = query_piece.shape[1]
    bias_part = bias_cols
    lse_piece = lse_all.transpose(0, 2, 1)
    delta_piece = delta_all.transpose(0, 2, 1)
    piece_heads = split_heads(query_piece)
    piece_grads = split_heads(grad_piece)
    logits = scores(piece_heads, key_heads_own, bias_part, own_keep)
    shares = jnp.exp(logits - lse_piece[..., None])
    grad_shares = jnp.einsum(
        "ijhd,ikhd->ihjk", piece_grads, value_heads_own, preferred_element_type=f32
    )
    grad_logits = shares * (grad_shares - delta_piece[..., None])
    grad_key = jnp.einsum(
        "ihjk,ijhd->ikhd", grad_logits.astype(bf16), piece_heads, preferred_element_type=f32
    )
    grad_value = jnp.einsum(
        "ihjk,ijhd->ikhd", shares.astype(bf16), piece_grads, preferred_element_type=f32
    )
    block_sum = grad_logits.sum(0)
    grad_key, grad_value, grad_bias_cols = (grad_key, grad_value, block_sum)
    grad_bias_tile = lax.psum_scatter(grad_bias_cols, "rows", scatter_dimension=1, tiled=True)
    flat_shape = (window_rows, cols_blk, channels)
    combined = jnp.concatenate(
        [
            (grad_query.reshape(flat_shape) * score_scale).astype(bf16),
            grad_key.reshape(flat_shape).astype(bf16),
            grad_value.reshape(flat_shape).astype(bf16),
            grad_pre.astype(bf16),
        ],
        axis=-1,
    )
    stacked = jnp.concatenate([w_query, w_key, w_value, w_gate], axis=1)
    grad_window = lax.dot_general(
        combined, stacked, (((2,), (1,)), ((), ())), preferred_element_type=f32
    )
    grad_normed = jnp.einsum(
        "hij,ch->ijc", grad_bias_tile, w_bias.astype(f32), precision=lax.Precision.HIGHEST
    )
    grad_normed = grad_normed.at[:window_rows].add(grad_window)
    unused, pullback = jax.vjp(lambda inputs: layer_norm(inputs, ln_gain), pair_f)
    pair_grad = pullback(grad_normed)[0]
    return (update, pair_grad)


def solution(mesh):
    placed = (
        P("rows", "cols", None),
        P(),
        P(),
        P(),
        P(),
        P(),
        P(),
        P(),
        P(),
        P("rows", "cols", None),
    )
    return jax.shard_map(
        body,
        mesh=mesh,
        in_specs=placed,
        out_specs=(P("rows", "cols", None), P("rows", "cols", None)),
        check_vma=False,
    )
```

profile of v0, /device:TPU:1, one launch (start us, length us, event | category | flops | bytes accessed | tf_op | source)
XLA Modules:
  0.0 774.4 jit_solution(5966728969735832759)
XLA Ops:
  12.0 1.9 fusion.44
  14.6 52.3 %all_gather.27 = bf16[4,64,1024]{1,0,2:T(4,128)(2,1)S(1)} all-gather(bf16[4,64,32]{1,0,2:T(4,128)(2,1)S(1)} %copy.90), channel_id=1, replica_groups=mesh['rows'=16,'cols'=32] {'cols'}, dimensions={2}, use_global_device_ids=true | all-gather | bytes 540672 | tf_op jit(solution)/shard_map/all_gather | solution.py:47
  74.6 183.5 %all-reduce.4.cloned.1.call-done = bf16[4,64,1024]{2,1,0:T(8,128)(2,1)} async-done(((bf16[4,64,1024]{2,1,0:T(8,128)(2,1)}), bf16[4,64,1024]{2,1,0:T(8,128)(2,1)}) %all-reduce.4.cloned.1.call-update) | async-done | bytes 524304 | tf_op jit(solution)/shard_map/psum | solution.py:12
  259.1 2.9 copy.88
  262.0 4.0 copy.92
  270.6 2.0 fusion.49
  273.8 2.0 multiply_convert_fusion.1
  276.7 1.7 reshape.128
  278.4 68.4 %all_gather.30 = bf16[4,1024,32]{2,0,1:T(4,128)(2,1)} all-gather(bf16[4,64,32]{2,0,1:T(4,128)(2,1)S(1)} %copy-done.13), channel_id=1, replica_groups=mesh['rows'=16,'cols'=32] {'rows'}, dimensions={1}, use_global_device_ids=true | all-gather | bytes 278528 | tf_op jit(solution)/shard_map/all_gather | solution.py:46
  352.7 1.8 multiply_reduce_fusion
  357.2 5.7 fusion.30
  362.9 1.7 copy.110
  364.7 69.9 %all_gather.31 = f32[8,1024,4]{0,2,1:T(4,128)S(1)} all-gather(f32[8,32,4]{0,2,1:T(4,128)S(1)} %copy.97), channel_id=1, replica_groups=mesh['rows'=16,'cols'=32] {'cols'}, dimensions={1}, use_global_device_ids=true | all-gather | bytes 135168 | tf_op jit(solution)/shard_map/all_gather | solution.py:102
  436.1 48.8 %all_gather.33 = f32[8,1024,4]{0,2,1:T(4,128)S(1)} all-gather(f32[8,32,4]{0,2,1:T(4,128)S(1)} %copy-done.11), channel_id=1, replica_groups=mesh['rows'=16,'cols'=32] {'cols'}, dimensions={1}, use_global_device_ids=true | all-gather | bytes 135168 | tf_op jit(solution)/shard_map/all_gather | solution.py:103
  486.3 2.9 copy.94
  490.0 2.6 fusion.61
  492.6 3.9 copy.99
  496.5 6.1 fusion.95
  502.7 1.7 copy.104
  504.4 4.0 fusion.34
  508.7 2.3 fusion.31
  511.1 249.3 %all-reduce.6.cloned.1.call-done = f32[4,1024,32]{2,0,1:T(4,128)} async-done(((f32[4,1024,32]{2,0,1:T(4,128)}), f32[4,1024,32]{2,0,1:T(4,128)}) %all-reduce.6.cloned.1.call-update) | async-done | bytes 524304
  760.4 1.9 fusion.71
  764.7 2.0 broadcast_add_fusion
  (121 shorter events, 33.5 us)
Async XLA Ops:
  8.0 65.7 %copy-start = (bf16[8,32,128]{2,1,0:T(8,128)(2,1)S(1)}, bf16[8,32,128]{2,1,0:T(8,128)(2,1)}, u32[]{:S(2)}) copy-start(bf16[8,32,128]{2,1,0:T(8,128)(2,1)} %param.21) | copy-start | bytes 196612
  8.0 60.5 %copy-start.2 = (bf16[64,32,128]{2,1,0:T(8,128)(2,1)S(1)}, bf16[64,32,128]{2,1,0:T(8,128)(2,1)}, u32[]{:S(2)}) copy-start(bf16[64,32,128]{2,1,0:T(8,128)(2,1)} %param.12) | copy-start | bytes 1572868
  8.0 60.5 %copy-start.21 = (f32[128]{0:T(128)S(1)}, f32[128]{0:T(128)}, u32[]{:S(2)}) copy-start(f32[128]{0:T(128)} %param.14) | copy-start | bytes 1540
  8.0 60.5 %copy-start.26 = (bf16[128,128]{1,0:T(8,128)(2,1)S(1)}, bf16[128,128]{1,0:T(8,128)(2,1)}, u32[]{:S(2)}) copy-start(bf16[128,128]{1,0:T(8,128)(2,1)} %param.16) | copy-start | bytes 98308
  8.0 61.5 %copy-start.28 = (bf16[128,128]{1,0:T(8,128)(2,1)S(1)}, bf16[128,128]{1,0:T(8,128)(2,1)}, u32[]{:S(2)}) copy-start(bf16[128,128]{1,0:T(8,128)(2,1)} %param.17) | copy-start | bytes 98308
  8.1 62.4 %copy-start.30 = (bf16[128,128]{1,0:T(8,128)(2,1)S(1)}, bf16[128,128]{1,0:T(8,128)(2,1)}, u32[]{:S(2)}) copy-start(bf16[128,128]{1,0:T(8,128)(2,1)} %param.15) | copy-start | bytes 98308
  8.1 65.7 %copy-start.17 = (bf16[128,128]{1,0:T(8,128)(2,1)S(1)}, bf16[128,128]{1,0:T(8,128)(2,1)}, u32[]{:S(2)}) copy-start(bf16[128,128]{1,0:T(8,128)(2,1)} %param.20) | copy-start | bytes 98308
  8.1 250.0 %all-reduce.4.cloned.1.call-start = ((), (), s32[]{:S(2)}) async-start(), calls=%async_computation.1 | async-start | bytes 1048576 | tf_op jit(solution)/shard_map/psum | solution.py:12
  68.5 190.6 %all-gather.5.cloned.1.call-start = ((), (), s32[]{:S(2)}) async-start(), calls=%async_computation | async-start | bytes 2162688 | tf_op jit(solution)/shard_map/all_gather | solution.py:61
  69.5 192.5 %all-gather.7.cloned.1.call-start = ((), (), s32[]{:S(2)}) async-start(), calls=%async_computation.2 | async-start | bytes 2162688 | tf_op jit(solution)/shard_map/all_gather | solution.py:62
  70.5 415.8 %all-gather.9.cloned.1.call-start = ((), (), s32[]{:S(2)}) async-start(), calls=%async_computation.3 | async-start | bytes 2162688 | tf_op jit(solution)/shard_map/all_gather | solution.py:108
  71.4 421.2 %all-gather.11.cloned.1.call-start = ((), (), s32[]{:S(2)}) async-start(), calls=%async_computation.4 | async-start | bytes 2162688 | tf_op jit(solution)/shard_map/all_gather | solution.py:109
  275.8 484.6 %all-reduce.6.cloned.1.call-start = ((), (), s32[]{:S(2)}) async-start(), calls=%async_computation.5 | async-start | bytes 4194304
  362.9 73.1 %copy-start.11 = (f32[8,32,4]{0,2,1:T(4,128)S(1)}, f32[8,32,4]{0,2,1:T(4,128)}, u32[]{:S(2)}) copy-start(f32[8,32,4]{0,2,1:T(4,128)} %copy.102) | copy-start | bytes 12292
  436.0 53.9 %copy-start.5 = (bf16[8,32,4,32]{3,2,1,0:T(4,128)(2,1)S(1)}, bf16[8,32,4,32]{3,2,1,0:T(4,128)(2,1)}, u32[]{:S(2)}) copy-start(bf16[8,32,4,32]{3,2,1,0:T(4,128)(2,1)} %reshape.126) | copy-start | bytes 196612
  508.4 252.0 %copy-start.24 = (bf16[128,4]{0,1:T(4,128)(2,1)S(1)}, bf16[128,4]{0,1:T(4,128)(2,1)}, u32[]{:S(2)}) copy-start(bf16[128,4]{0,1:T(4,128)(2,1)} %param.19) | copy-start | bytes 3076
  508.5 253.9 %copy-start.19 = (bf16[8,32,128]{2,1,0:T(8,128)(2,1)S(1)}, bf16[8,32,128]{2,1,0:T(8,128)(2,1)}, u32[]{:S(2)}) copy-start(bf16[8,32,128]{2,1,0:T(8,128)(2,1)} %copy.110) | copy-start | bytes 196612
  508.5 253.9 %copy-start.27 = (bf16[128,128]{1,0:T(8,128)(2,1)S(1)}, bf16[128,128]{1,0:T(8,128)(2,1)}, u32[]{:S(2)}) copy-start(bf16[128,128]{1,0:T(8,128)(2,1)} %param.16) | copy-start | bytes 98308
  508.5 253.9 %copy-start.29 = (bf16[128,128]{1,0:T(8,128)(2,1)S(1)}, bf16[128,128]{1,0:T(8,128)(2,1)}, u32[]{:S(2)}) copy-start(bf16[128,128]{1,0:T(8,128)(2,1)} %param.17) | copy-start | bytes 98308
  508.5 253.9 %copy-start.31 = (bf16[128,128]{1,0:T(8,128)(2,1)S(1)}, bf16[128,128]{1,0:T(8,128)(2,1)}, u32[]{:S(2)}) copy-start(bf16[128,128]{1,0:T(8,128)(2,1)} %param.15) | copy-start | bytes 98308
  508.5 253.9 %copy-start.32 = (bf16[128,128]{1,0:T(8,128)(2,1)S(1)}, bf16[128,128]{1,0:T(8,128)(2,1)}, u32[]{:S(2)}) copy-start(bf16[128,128]{1,0:T(8,128)(2,1)} %param.18) | copy-start | bytes 98308
  508.5 253.9 %copy-start.33 = (bf16[8,32,128]{2,1,0:T(8,128)(2,1)S(1)}, bf16[8,32,128]{2,1,0:T(8,128)(2,1)}, u32[]{:S(2)}) copy-start(bf16[8,32,128]{2,1,0:T(8,128)(2,1)} %get-tuple-element.14) | copy-start | bytes 196612
  508.5 254.2 %copy-start.22 = (f32[128]{0:T(128)S(1)}, f32[128]{0:T(128)}, u32[]{:S(2)}) copy-start(f32[128]{0:T(128)} %param.14) | copy-start | bytes 1540
  508.7 254.7 %copy-start.10 = (f32[64,32]{1,0:T(8,128)S(1)}, f32[64,32]{1,0:T(8,128)}, u32[]{:S(2)}) copy-start(f32[64,32]{1,0:T(8,128)} %copy-done.9) | copy-start | bytes 24580
  (16 other events, 214.4 us)
Sparse Core Ops, SparseCore 0:
  68.6 189.3 all-reduce.3
  504.6 255.8 all-reduce.5
Sparse Core Ops, SparseCore 1:
  71.1 63.3 all-gather.4
  137.1 62.1 all-gather.6
  201.6 62.7 all-gather.8
  275.9 81.0 all-gather.10
where the time goes:
time: 785 us; the launch traced here: 774 us
  waiting for transfers between devices  433 us (55%)
  blocking collectives  239 us (30%)
  matrix products  34.5 us (4%)
  local copies, waits for them, and re-layouts  33.7 us (4%)
  between operations  17.6 us (2%)
  other arithmetic  15.9 us (2%)
    unnamed x7, waiting for transfers between devices  249 us
    psum x1, waiting for transfers between devices, broadcast(): return lax.psum(kept, axis)  183 us
    all_gather x1, blocking collectives, body(): lax.all_gather(lse.transpose(0, 2, 1), 'cols', axis=1, tiled=True)  69.9 us
    all_gather x1, blocking collectives, body(): bias_cols = lax.all_gather(bias_tile, 'rows', axis=1, tiled=True)  68.4 us
    all_gather x1, blocking collectives, body(): bias_band = lax.all_gather(bias_tile, 'cols', axis=2, tiled=True)  52.3 us
    all_gather x1, blocking collectives, body(): lax.all_gather(delta, 'cols', axis=1, tiled=True)  48.8 us
  transfers between devices with their start and end apart: 6, of which 2 were waited for; matrix products, arithmetic and copies ran while one was open for 7% of the time, Pallas kernels for 0%

commit v1 on v0

v1 whole, which is shorter than its diff:
```python
import jax
import jax.numpy as jnp
from jax import lax
from jax.experimental import pallas as pl
from jax.experimental.pallas import tpu as pltpu
from jax.sharding import PartitionSpec as P

EPS = 1e-05
NEG = -1000000000.0
MESH = pl.DeviceIdType.MESH
f32 = jnp.float32
bf16 = jnp.bfloat16


def nn(left, right):
    return lax.dot_general(left, right, (((1,), (0,)), ((), ())), preferred_element_type=f32)


def nt(left, right):
    return lax.dot_general(left, right, (((1,), (1,)), ((), ())), preferred_element_type=f32)


def lane_block(shape):
    return lax.shift_right_logical(lax.broadcasted_iota(jnp.int32, shape, len(shape) - 1), 5)


def lane_swap(tiles):
    block = lane_block(tiles[0].shape)
    outs = []
    for i in range(4):
        acc = None
        for b in range(4):
            shift = (32 * (b - i)) % 128
            moved = tiles[b] if shift == 0 else pltpu.roll(tiles[b], shift, 1)
            acc = moved if acc is None else jnp.where(block == b, moved, acc)
        outs.append(acc)
    return outs


def remote(src, dst, send_sem, recv_sem, device):
    return pltpu.make_async_remote_copy(
        src_ref=src, dst_ref=dst, send_sem=send_sem, recv_sem=recv_sem,
        device_id=device, device_id_type=MESH,
    )


def kernel(
    pair, length, gain, w_query, w_key, w_value, w_gate, w_bias, w_out, out_grad,
    update, pair_grad,
    xhat, rstd_all, w_rows, gate_s, gg_s, zsend, kv, qd, qdt, bsend, brecv, grid, bias, bias_f,
    dbias, att, dqkv, db_send, db_x, db_y, db_t, db_h, db_out, db_in, dkv_send, dkv_in,
    e_in, o_in, gw,
    kvz_s, kvz_r, qdz_s, qdz_r, bz_s, bz_r, kvx_s, kvx_r, kvc_s, kvc_r, bh_s, bh_r,
    by_s, by_r, by2_s, by2_r, bx_s, bx_r, dbx_s, dbx_r, dby_s, dby_r, dbh_s, dbh_r,
    dbz_s, dbz_r, dkvx_s, dkvx_r, oz_s, oz_r, dqz_s, dqz_r, dkvz_s, dkvz_r,
):
    row = lax.axis_index("rows")
    col = lax.axis_index("cols")
    y, zhi = lax.div(row, 2), lax.rem(row, 2)
    x, z, core = lax.div(col, 8), lax.rem(lax.div(col, 2), 4), lax.rem(col, 2)
    blk = x * 2 + core
    other = 1 - core

    def device(row_, x_, z_, core_):
        return {"rows": row_, "cols": x_ * 8 + z_ * 2 + core_}

    def z_at(d):
        return lax.rem(z + d, 4)

    def z_dev(d):
        return device(row, x, z_at(d), core)

    def x_at(d):
        return lax.rem(x + d, 4)

    def x_dev(d):
        return device(row, x_at(d), z, core)

    def blk_at(d):
        return lax.rem(blk + d, 8)

    def blk_dev(d):
        return device(row, lax.div(blk_at(d), 2), z, lax.rem(blk_at(d), 2))

    def y_at(d):
        return lax.rem(y + d, 8)

    def y_dev(d):
        return device(y_at(d) * 2 + zhi, x, z, core)

    core_dev = device(row, x, z, other)
    h_dev = device(y * 2 + 1 - zhi, x, z, core)
    me_dev = core_dev

    sent = []

    def send(src, dst, send_sem, recv_sem, dev):
        copy = remote(src, dst, send_sem, recv_sem, dev)
        copy.start()
        sent.append(copy)

    def arrived(slot, send_sem, recv_sem):
        remote(slot, slot, send_sem, recv_sem, me_dev).wait_recv()

    barrier = pltpu.get_barrier_semaphore()
    partners = (
        [z_dev(d) for d in (1, 2, 3)] + [blk_dev(d) for d in range(1, 8)]
        + [y_dev(d) for d in range(1, 8)] + [h_dev]
    )
    for dev in partners:
        pl.semaphore_signal(barrier, inc=1, device_id=dev, device_id_type=MESH)

    gain_v = gain[...]

    def norm(values):
        average = jnp.mean(values, axis=-1, keepdims=True)
        centred = values - average
        variance = jnp.mean(centred * centred, axis=-1, keepdims=True)
        rstd = lax.rsqrt(variance + EPS)
        return centred * rstd, rstd, centred

    win = pair[0:8].reshape(256, 128).astype(f32)
    hat, _, _ = norm(win)
    window = (hat * gain_v).astype(bf16)
    query = (nn(window, w_query[...]) * (32 ** (-0.5))).astype(bf16).astype(f32)
    keys = nn(window, w_key[...]).astype(bf16).astype(f32)
    vals = nn(window, w_value[...]).astype(bf16).astype(f32)
    gate = jax.nn.sigmoid(nn(window, w_gate[...])).astype(bf16).astype(f32)
    gg = nt(out_grad[...].reshape(256, 128), w_out[...])
    ga = (gg * gate).astype(bf16).astype(f32)
    gate_s[...] = gate
    gg_s[...] = gg
    for n, array in enumerate((keys, vals, query, ga)):
        for g in range(2):
            outs = lane_swap([array[(g * 4 + b) * 32:(g * 4 + b + 1) * 32] for b in range(4)])
            for h in range(4):
                zsend[h, n, g] = outs[h].astype(bf16)

    pl.semaphore_wait(barrier, len(partners))

    z_rows = pl.ds(pl.multiple_of(z * 32, 32), 32)
    for d in (1, 3, 2):
        send(zsend.at[z_at(d), 0:2], kv.at[blk, :, :, z_rows, :], kvz_s.at[d], kvz_r.at[d], z_dev(d))
    for d in (1, 3, 2):
        send(zsend.at[z_at(d), 2:4], qd.at[:, :, z_rows, :], qdz_s.at[d], qdz_r.at[d], z_dev(d))
    kv[blk, :, :, z_rows, :] = zsend[z, 0:2]
    qd[:, :, z_rows, :] = zsend[z, 2:4]

    pick = lax.broadcasted_iota(jnp.int32, (64, 4), 0) // 16 == lax.broadcasted_iota(
        jnp.int32, (64, 4), 1)
    w_rows[...] = nt(pick.astype(bf16), w_bias[...]).astype(bf16)
    row_in = lax.rem(lax.broadcasted_iota(jnp.int32, (64, 128), 0), 16)

    def tile_step(i, acc):
        for u in range(4):
            jj = i * 4 + u
            tokens = jnp.concatenate([pair[q * 16 + jj] for q in range(4)], axis=0).astype(f32)
            hat, rstd, _ = norm(tokens)
            xhat[jj] = hat
            rstd_all[jj] = jnp.broadcast_to(rstd, (128, 128))
            normed = (hat * gain_v).astype(bf16)
            chosen = jnp.where(row_in == jj, w_rows[...].astype(f32), 0.0).astype(bf16)
            acc = acc + nt(chosen, normed)
        return acc

    tile_bias = lax.fori_loop(0, 4, tile_step, jnp.zeros((64, 128), f32))
    bsend[...] = tile_bias.astype(bf16).reshape(4, 16, 128)
    for d in (1, 3, 2):
        send(bsend.at[z_at(d)], brecv.at[z], bz_s.at[d], bz_r.at[d], z_dev(d))
    brecv[z] = bsend[z]

    for d in (1, 2, 3):
        rows_d = pl.ds(pl.multiple_of(z_at(4 - d) * 32, 32), 32)
        arrived(kv.at[blk, :, :, rows_d, :], kvz_s.at[d], kvz_r.at[d])
    for d in (1, 3, 2):
        send(kv.at[blk], kv.at[blk], kvx_s.at[d], kvx_r.at[d], x_dev(d))
    send(kv.at[blk], kv.at[blk], kvc_s.at[0], kvc_r.at[0], core_dev)

    for d in (1, 2, 3):
        arrived(brecv.at[z_at(4 - d)], bz_s.at[d], bz_r.at[d])
    outs = lane_swap([brecv[b].astype(f32) for b in range(4)])
    for q in range(4):
        grid[row, q * 16:(q + 1) * 16] = outs[q].astype(bf16)
    send(grid.at[row], grid.at[row], bh_s.at[0], bh_r.at[0], h_dev)
    for d in (1, 7, 2, 6, 3, 5, 4):
        send(grid.at[row], grid.at[row], by_s.at[d], by_r.at[d], y_dev(d))
    row_h = y * 2 + 1 - zhi
    arrived(grid.at[row_h], bh_s.at[0], bh_r.at[0])
    for d in (1, 7, 2, 6, 3, 5, 4):
        send(grid.at[row_h], grid.at[row_h], by2_s.at[d], by2_r.at[d], y_dev(d))

    for d in (1, 2, 3):
        rows_d = pl.ds(pl.multiple_of(z_at(4 - d) * 32, 32), 32)
        arrived(qd.at[:, :, rows_d, :], qdz_s.at[d], qdz_r.at[d])
    for n in range(2):
        for g in range(2):
            qdt[n, g] = qd[n, g].astype(f32).T.astype(bf16)

    for d in range(1, 8):
        arrived(grid.at[y_at(8 - d) * 2 + zhi], by_s.at[d], by_r.at[d])
        arrived(grid.at[y_at(8 - d) * 2 + 1 - zhi], by2_s.at[d], by2_r.at[d])
    for d in (1, 7, 2, 6, 3, 5, 4):
        to = blk_at(d)
        part = grid.at[
            pl.ds(pl.multiple_of(lax.div(to, 2) * 4, 4), 4),
            pl.ds(pl.multiple_of(lax.rem(to, 2) * 32, 32), 32), :]
        send(part, bias.at[blk], bx_s.at[d], bx_r.at[d], blk_dev(d))
    bias[blk] = grid[pl.ds(pl.multiple_of(x * 4, 4), 4), pl.ds(pl.multiple_of(core * 32, 32), 32), :]

    for d in (1, 3, 2):
        blk_d = x_at(4 - d) * 2 + core
        arrived(kv.at[blk_d], kvx_s.at[d], kvx_r.at[d])
        send(kv.at[blk_d], kv.at[blk_d], kvc_s.at[d], kvc_r.at[d], core_dev)
    for d in (0, 1, 3, 2):
        arrived(kv.at[x_at(4 - d) * 2 + other], kvc_s.at[d], kvc_r.at[d])
    for d in range(1, 8):
        arrived(bias.at[blk_at(8 - d)], bx_s.at[d], bx_r.at[d])

    spot = lax.broadcasted_iota(jnp.int32, (1, 1024), 1)
    spot_c = (lax.div(spot, 256) * 8 + lax.rem(lax.div(spot, 32), 4) * 2
              + lax.rem(lax.div(spot, 128), 2))
    keep = spot_c * 32 + lax.rem(spot, 32) < length[0]
    for b in range(8):
        bias_f[:, b * 128:(b + 1) * 128] = bias[b].reshape(128, 128).astype(f32)
    dbias[...] = jnp.zeros_like(dbias)
    att[...] = jnp.zeros_like(att)
    dqkv[0] = jnp.zeros_like(dqkv[0])
    lanes = lane_block((128, 128))

    for g in range(2):
        def attend(a, carry):
            own = lanes == a
            key = kv[:, 0, g].reshape(1024, 128)
            value = kv[:, 1, g].reshape(1024, 128)
            q_a = jnp.where(own, qd[0, g].astype(f32), 0.0).astype(bf16)
            do_f = jnp.where(own, qd[1, g].astype(f32), 0.0)
            do_a = do_f.astype(bf16)
            logits = jnp.where(keep, nt(q_a, key) + bias_f[...], NEG)
            top = jnp.max(logits, axis=-1, keepdims=True)
            expo = jnp.exp(logits - top)
            inv = 1.0 / jnp.sum(expo, axis=-1, keepdims=True)
            out = nn(expo.astype(bf16), value) * inv
            out = jnp.where(own, out, 0.0)
            att[g] = att[g] + out
            delta = jnp.sum(do_f * out, axis=-1, keepdims=True)
            shares = expo * inv
            grads = shares * (nt(do_a, value) - delta)
            dbias[...] = dbias[...] + grads
            grads_b = grads.astype(bf16)
            dq = nn(grads_b, key) * (32 ** (-0.5))
            dqkv[0, g] = jnp.where(own, dq, dqkv[0, g].astype(f32)).astype(bf16)
            part = pl.ds(pl.multiple_of(a * 32, 32), 32)
            dk = nn(qdt[0, g, part, :], grads_b).astype(bf16)
            dv = nn(qdt[1, g, part, :], shares.astype(bf16)).astype(bf16)
            for b in range(8):
                dkv_send[b, 0, g, part, :] = dk[:, b * 128:(b + 1) * 128]
                dkv_send[b, 1, g, part, :] = dv[:, b * 128:(b + 1) * 128]
            return carry

        lax.fori_loop(0, 4, attend, 0)

    for b in range(8):
        db_send[b] = dbias[:, b * 128:(b + 1) * 128].astype(bf16)
    for d in (1, 7, 2, 6, 3, 5, 4):
        send(db_send.at[blk_at(d)], db_x.at[blk], dbx_s.at[d], dbx_r.at[d], blk_dev(d))
    for d in (1, 7, 2, 6, 3, 5, 4):
        send(dkv_send.at[blk_at(d)], dkv_in.at[blk], dkvx_s.at[d], dkvx_r.at[d], blk_dev(d))
    for d in (1, 3, 2):
        rows_d = pl.ds(pl.multiple_of(z_at(d) * 32, 32), 32)
        send(att.at[:, rows_d, :], o_in.at[z], oz_s.at[d], oz_r.at[d], z_dev(d))
        send(dqkv.at[0, :, rows_d, :], e_in.at[z, 0], dqz_s.at[d], dqz_r.at[d], z_dev(d))
    db_x[blk] = db_send[blk]
    dkv_in[blk] = dkv_send[blk]
    o_in[z] = att[:, z_rows, :]
    e_in[z, 0] = dqkv[0, :, z_rows, :]

    for d in range(1, 8):
        arrived(db_x.at[blk_at(8 - d)], dbx_s.at[d], dbx_r.at[d])

    def y_part(to):
        return (pl.ds(pl.multiple_of(lax.div(to, 2) * 2, 2), 2),
                pl.ds(pl.multiple_of(lax.rem(to, 2) * 64, 64), 64))

    for d in (1, 7, 2, 6, 3, 5, 4):
        blks, js = y_part(y_at(d))
        send(db_x.at[blks, js, :], db_y.at[y], dby_s.at[d], dby_r.at[d], y_dev(d))
    blks, js = y_part(y)
    db_y[y] = db_x[blks, js, :]

    for d in range(1, 8):
        arrived(db_y.at[y_at(8 - d)], dby_s.at[d], dby_r.at[d])
    total = db_y[0].astype(f32)
    for b in range(1, 8):
        total = total + db_y[b].astype(f32)
    db_t[...] = total
    theirs = pl.ds(pl.multiple_of((1 - zhi) * 32, 32), 32)
    mine = pl.ds(pl.multiple_of(zhi * 32, 32), 32)
    send(db_t.at[:, theirs, :], db_h, dbh_s.at[0], dbh_r.at[0], h_dev)

    for d in range(1, 8):
        arrived(dkv_in.at[blk_at(8 - d)], dkvx_s.at[d], dkvx_r.at[d])
    for n in range(2):
        for g in range(2):
            total = dkv_in[0, n, g].astype(f32)
            for b in range(1, 8):
                total = total + dkv_in[b, n, g].astype(f32)
            dqkv[1 + n, g] = total.T.astype(bf16)
    for d in (1, 3, 2):
        rows_d = pl.ds(pl.multiple_of(z_at(d) * 32, 32), 32)
        send(dqkv.at[1:3, :, rows_d, :], e_in.at[z, 1:3], dkvz_s.at[d], dkvz_r.at[d], z_dev(d))
    e_in[z, 1:3] = dqkv[1:3, :, z_rows, :]

    arrived(db_h, dbh_s.at[0], dbh_r.at[0])
    final = (db_t[:, mine, :] + db_h[...]).reshape(64, 128)
    outs = lane_swap([final[q * 16:(q + 1) * 16] for q in range(4)])
    for b in range(4):
        db_out[b] = outs[b]
    for d in (1, 3, 2):
        send(db_out.at[z_at(d)], db_in.at[z], dbz_s.at[d], dbz_r.at[d], z_dev(d))
    db_in[z] = db_out[z]

    for d in (1, 2, 3):
        h_d = z_at(4 - d)
        arrived(o_in.at[h_d], oz_s.at[d], oz_r.at[d])
        arrived(e_in.at[h_d, 0], dqz_s.at[d], dqz_r.at[d])
    gated = []
    pres = []
    for g in range(2):
        outs = lane_swap([o_in[h, g] for h in range(4)])
        for i in range(4):
            at = slice((g * 4 + i) * 32, (g * 4 + i + 1) * 32)
            gate_t, gg_t = gate_s[at], gg_s[at]
            gated.append((gate_t * outs[i]).astype(bf16))
            pres.append((gg_t * outs[i] * gate_t * (1.0 - gate_t)).astype(bf16))
    update[...] = nn(jnp.concatenate(gated, axis=0), w_out[...]).astype(bf16).reshape(8, 32, 128)
    for d in (1, 2, 3):
        arrived(e_in.at[z_at(4 - d), 1:3], dkvz_s.at[d], dkvz_r.at[d])
    sides = [jnp.concatenate(pres, axis=0)]
    for n in range(3):
        tiles = []
        for g in range(2):
            tiles += lane_swap([e_in[h, n, g].astype(f32) for h in range(4)])
        sides.append(jnp.concatenate(tiles, axis=0).astype(bf16))
    grad_window = (nt(sides[1], w_query[...]) + nt(sides[2], w_key[...])
                   + nt(sides[3], w_value[...]) + nt(sides[0], w_gate[...]))
    gw[0:8] = grad_window.reshape(8, 32, 128)
    gw[8:16] = jnp.zeros((8, 32, 128), f32)

    for d in (1, 2, 3):
        arrived(db_in.at[z_at(4 - d)], dbz_s.at[d], dbz_r.at[d])
    flat = db_in[...].reshape(64, 128).T
    high = flat.astype(bf16)
    rest = flat - high.astype(f32)
    mid = rest.astype(bf16)
    low = (rest - mid.astype(f32)).astype(bf16)

    def final_step(i, carry):
        for u in range(2):
            jj = i * 2 + u
            chosen = jnp.where(row_in == jj, w_rows[...].astype(f32), 0.0).astype(bf16)
            grad = nn(high, chosen) + (nn(mid, chosen) + nn(low, chosen))
            grad = jnp.concatenate([grad[0:32] + gw[jj], grad[32:]], axis=0) * gain_v
            hat = xhat[jj]
            first = jnp.mean(grad, axis=-1, keepdims=True)
            second = jnp.mean(grad * hat, axis=-1, keepdims=True)
            result = rstd_all[jj] * (grad - first - hat * second)
            for q in range(4):
                pair_grad[q * 16 + jj] = result[q * 32:(q + 1) * 32]
        return carry

    lax.fori_loop(0, 8, final_step, 0)

    for copy in sent:
        copy.wait_send()


def body(pair, length, ln_gain, w_query, w_key, w_value, w_gate, w_bias, w_out, out_grad):
    vmem = pl.BlockSpec(memory_space=pltpu.VMEM)
    smem = pl.BlockSpec(memory_space=pltpu.SMEM)

    def dma(n):
        return [pltpu.SemaphoreType.DMA((n,)), pltpu.SemaphoreType.DMA((n,))]

    scratch = [
        pltpu.VMEM((16, 128, 128), f32),
        pltpu.VMEM((16, 128, 128), f32),
        pltpu.VMEM((64, 128), bf16),
        pltpu.VMEM((256, 128), f32),
        pltpu.VMEM((256, 128), f32),
        pltpu.VMEM((4, 4, 2, 32, 128), bf16),
        pltpu.VMEM((8, 2, 2, 128, 128), bf16),
        pltpu.VMEM((2, 2, 128, 128), bf16),
        pltpu.VMEM((2, 2, 128, 128), bf16),
        pltpu.VMEM((4, 16, 128), bf16),
        pltpu.VMEM((4, 16, 128), bf16),
        pltpu.VMEM((16, 64, 128), bf16),
        pltpu.VMEM((8, 4, 32, 128), bf16),
        pltpu.VMEM((128, 1024), f32),
        pltpu.VMEM((128, 1024), f32),
        pltpu.VMEM((2, 128, 128), f32),
        pltpu.VMEM((3, 2, 128, 128), bf16),
        pltpu.VMEM((8, 128, 128), bf16),
        pltpu.VMEM((8, 128, 128), bf16),
        pltpu.VMEM((8, 2, 64, 128), bf16),
        pltpu.VMEM((2, 64, 128), f32),
        pltpu.VMEM((2, 32, 128), f32),
        pltpu.VMEM((4, 16, 128), f32),
        pltpu.VMEM((4, 16, 128), f32),
        pltpu.VMEM((8, 2, 2, 128, 128), bf16),
        pltpu.VMEM((8, 2, 2, 128, 128), bf16),
        pltpu.VMEM((4, 3, 2, 32, 128), bf16),
        pltpu.VMEM((4, 2, 32, 128), f32),
        pltpu.VMEM((16, 32, 128), f32),
    ]
    for n in (4, 4, 4, 4, 4, 1, 8, 8, 8, 8, 8, 1, 4, 8, 4, 4, 4):
        scratch += dma(n)
    call = pl.pallas_call(
        kernel,
        out_shape=(
            jax.ShapeDtypeStruct(out_grad.shape, bf16),
            jax.ShapeDtypeStruct(pair.shape, f32),
        ),
        in_specs=[vmem, smem] + [vmem] * 8,
        out_specs=(vmem, vmem),
        scratch_shapes=scratch,
        compiler_params=pltpu.CompilerParams(
            collective_id=0, has_side_effects=True, vmem_limit_bytes=48 * 1024 * 1024
        ),
    )
    return call(
        pair, length, ln_gain.reshape(1, 128), w_query, w_key, w_value, w_gate, w_bias, w_out,
        out_grad,
    )


def solution(mesh):
    tiled = P("rows", "cols", None)
    placed = (tiled, P(), P(), P(), P(), P(), P(), P(), P(), tiled)
    return jax.shard_map(
        body, mesh=mesh, in_specs=placed, out_specs=(tiled, tiled), check_vma=False
    )
```

time: 785 us -> 79.4 us (0.10); the launches traced: 774 us -> 78.4 us
  waiting for transfers between devices: 433 us -> 0 us
  blocking collectives: 239 us -> 0 us
  Pallas kernels: 0 us -> 69.8 us
  matrix products: 34.5 us -> 0 us
  local copies, waits for them, and re-layouts: 33.7 us -> 7.33 us
  between operations: 17.6 us -> 1.33 us
  other arithmetic: 15.9 us -> 0 us
    unnamed x7 -> x0, waiting for transfers between devices: 249 us -> none
    all_gather x4 -> x0, blocking collectives: 239 us -> none  [the longest x1 69.9 us: body(): lax.all_gather(lse.transpose(0, 2, 1), 'cols', axis=1, tiled=True)]
    psum x1 -> x0, waiting for transfers between devices: 183 us -> none  [broadcast(): return lax.psum(kept, axis)]
    pallas_call x0 -> x1, Pallas kernels: none -> 69.8 us  [body(): call(pair, length, ln_gain.reshape(1, 128), w_query, w_key, w_value, w_ga...]
    dot_general x16 -> x0, matrix products: 34.5 us -> none  [the longest x1 6.15 us: body(): jnp.einsum('ijhd,ikhd->ihjk', piece_grads, value_heads_own, preferred_ele...]
    all_gather x6 -> x0, local copies, waits for them, and re-layouts: 15.7 us -> none  [the longest x1 3.96 us: body(): value_piece = lax.all_gather(value_proj, 'cols', axis=1, tiled=True)]
    reduce_sum x6 -> x0, other arithmetic: 7.92 us -> none  [the longest x1 1.76 us: body(): jnp.sum(split_heads(grad_attn).astype(f32) * split_heads(attended), -1)]
  transfers between devices with their start and end apart: 6 -> 0, of which waited for: 2 -> 0; matrix products, arithmetic and copies ran while one was open for 7% -> 0% of each run, Pallas kernels for 0% -> 0%
where the time goes in v1:
time: 79.4 us; the launch traced here: 78.4 us
  Pallas kernels  69.8 us (88%)
  local copies, waits for them, and re-layouts  7.33 us (9%)
  between operations  1.33 us (2%)
    pallas_call x1, Pallas kernels, body(): call(pair, length, ln_gain.reshape(1, 128), w_query, w_key, w_value, w_ga...  69.8 us
    unnamed x19, local copies, waits for them, and re-layouts  7.33 us

profile of v1, /device:TPU:1, one launch (start us, length us, event | category | flops | bytes accessed | tf_op | source)
XLA Modules:
  0.0 78.4 jit_solution(8336369533469684324)
XLA Ops:
  0.6 0.0 copy-start.2
  1.3 0.0 copy-start.7
  1.3 0.8 %copy.12.w_bias = bf16[128,4]{1,0:T(8,128)(2,1)S(1)} copy(bf16[128,4]{0,1:T(4,128)(2,1)} %param.17) | data formatting | bytes 2048 | tf_op args[7]
  2.1 0.0 copy-done.2
  2.1 0.0 copy-done.7
  2.1 0.0 copy-start
  2.1 1.0 %copy-done = bf16[64,32,128]{2,1,0:T(8,128)(2,1)S(1)} copy-done((bf16[64,32,128]{2,1,0:T(8,128)(2,1)S(1)}, bf16[64,32,128]{2,1,0:T(8,128)(2,1)}, u32[]{:S(2)}) %copy-start) | copy-done | bytes 524312
  3.2 0.0 copy-start.1
  3.2 0.8 %copy-done.1 = bf16[8,32,128]{2,1,0:T(8,128)(2,1)S(1)} copy-done((bf16[8,32,128]{2,1,0:T(8,128)(2,1)S(1)}, bf16[8,32,128]{2,1,0:T(8,128)(2,1)}, u32[]{:S(2)}) %copy-start.1) | copy-done | bytes 65560
  4.0 0.0 copy-start.3
  4.0 0.8 copy-done.3
  4.8 0.0 copy-start.4
  4.8 0.8 copy-done.4
  5.5 0.0 copy-start.5
  5.5 0.8 copy-done.5
  6.3 0.0 copy-start.6
  6.3 0.8 copy-done.6
  7.0 69.8 %shard_map.113 = (bf16[8,32,128]{2,1,0:T(8,128)(2,1)S(1)}, f32[64,32,128]{2,1,0:T(8,128)S(1)}) custom-call(bf16[64,32,128]{2,1,0:T(8,128)(2,1)S(1)} %copy-done, s32[1]{0:T(128)S(6)} %copy.15.length, f32[1,128]{1,0:T(1,128)S(1)} %bitcast.1, bf16[128,128]{1,0:T(8,128)(2,1)S(1)} %copy-done.2, bf16[128,128]{1,0:T(8,128)(2,1)S(1)} %copy-done.3, ...), custom_call_target="tpu_custom_call" | custom-call | tf_op jit(solution)/shard_map/pallas_call | solution.py:430
  76.8 0.6 copy.16
  77.4 1.0 %copy.17 = f32[64,32,128]{2,1,0:T(8,128)} copy(f32[64,32,128]{2,1,0:T(8,128)S(1)} %get-tuple-element.5) | data formatting | bytes 2097152
Async XLA Ops:
  0.6 1.5 %copy-start.2 = (bf16[128,128]{1,0:T(8,128)(2,1)S(1)}, bf16[128,128]{1,0:T(8,128)(2,1)}, u32[]{:S(2)}) copy-start(bf16[128,128]{1,0:T(8,128)(2,1)} %w_query.1) | copy-start | bytes 98308
  1.3 0.8 %copy-start.7 = (f32[128]{0:T(128)S(1)}, f32[128]{0:T(128)}, u32[]{:S(2)}) copy-start(f32[128]{0:T(128)} %param.12) | copy-start | bytes 1540
  2.1 1.0 %copy-start = (bf16[64,32,128]{2,1,0:T(8,128)(2,1)S(1)}, bf16[64,32,128]{2,1,0:T(8,128)(2,1)}, u32[]{:S(2)}) copy-start(bf16[64,32,128]{2,1,0:T(8,128)(2,1)} %pair.1) | copy-start | bytes 1572868
  3.2 0.8 %copy-start.1 = (bf16[8,32,128]{2,1,0:T(8,128)(2,1)S(1)}, bf16[8,32,128]{2,1,0:T(8,128)(2,1)}, u32[]{:S(2)}) copy-start(bf16[8,32,128]{2,1,0:T(8,128)(2,1)} %out_grad.1) | copy-start | bytes 196612
  4.0 0.8 copy-start.3
  4.8 0.8 copy-start.4
  5.5 0.8 copy-start.5
  6.3 0.8 copy-start.6

commit v2 on v1

v2 whole, which is shorter than its diff:
```python
import jax
import jax.numpy as jnp
from jax import lax
from jax.experimental import pallas as pl
from jax.experimental.pallas import tpu as pltpu
from jax.sharding import PartitionSpec as P

EPS = 1e-05
NEG = -1000000000.0
MESH = pl.DeviceIdType.MESH
f32 = jnp.float32
bf16 = jnp.bfloat16
COPIES = (
    ("kvz", 4), ("qdz", 4), ("bz", 8), ("kva", 4), ("kvb", 2), ("kvc", 4), ("bt", 2), ("ya", 8),
    ("yb", 2), ("dkvc", 2), ("dr", 4), ("df", 8), ("yr", 4), ("yd", 4), ("dt", 2), ("dbz", 8),
    ("oz", 4), ("dqz", 4), ("dkvz", 4),
)


def nn(left, right):
    return lax.dot_general(left, right, (((1,), (0,)), ((), ())), preferred_element_type=f32)


def nt(left, right):
    return lax.dot_general(left, right, (((1,), (1,)), ((), ())), preferred_element_type=f32)


def lane_block(shape):
    return lax.shift_right_logical(lax.broadcasted_iota(jnp.int32, shape, len(shape) - 1), 5)


def lane_swap(tiles):
    block = lane_block(tiles[0].shape)
    outs = []
    for i in range(4):
        acc = None
        for b in range(4):
            shift = (32 * (b - i)) % 128
            moved = tiles[b] if shift == 0 else pltpu.roll(tiles[b], shift, 1)
            acc = moved if acc is None else jnp.where(block == b, moved, acc)
        outs.append(acc)
    return outs


def remote(src, dst, send_sem, recv_sem, device):
    return pltpu.make_async_remote_copy(
        src_ref=src, dst_ref=dst, send_sem=send_sem, recv_sem=recv_sem,
        device_id=device, device_id_type=MESH,
    )


def kernel(
    pair_h, length, gain, w_query_h, w_key_h, w_value_h, w_gate_h, w_bias, w_out_h, out_grad_h,
    update, pair_grad,
    pair, w_query, w_key, w_value, w_gate, w_out, out_grad, load_sem, xhat, rstd_all, w_rows, gate_s, gg_s, zsend, kv, qd, qdt, bsend, brecv, grid, bias, bias_f,
    dbias, att, dqkv, db_send, db_r, db_rh, db_2, db_y, db_s, db_t, db_out, db_in,
    dkv_send, dkv_c, dkv_m, dkv_r, dkv_2, dkv_in,
    e_in, o_in, gw,
    *sems,
):
    sem = {name: sems[2 * n:2 * n + 2] for n, (name, _) in enumerate(COPIES)}
    row = lax.axis_index("rows")
    col = lax.axis_index("cols")
    y, zhi = lax.div(row, 2), lax.rem(row, 2)
    x, z, core = lax.div(col, 8), lax.rem(lax.div(col, 2), 4), lax.rem(col, 2)
    blk = x * 2 + core
    other = 1 - core

    def device(row_, x_, z_, core_):
        return {"rows": row_, "cols": x_ * 8 + z_ * 2 + core_}

    def z_at(d):
        return lax.rem(z + d, 4)

    def z_dev(d):
        return device(row, x, z_at(d), core)

    def zz_dev(e, d):
        return device(y * 2 + lax.rem(zhi + e, 2), x, z_at(d), core)

    def x_at(d):
        return lax.rem(x + d, 4)

    def x_dev(d):
        return device(row, x_at(d), z, core)

    def y_at(d):
        return lax.rem(y + d, 8)

    def y_dev(d):
        return device(y_at(d) * 2 + zhi, x, z, core)

    def by_column(c):
        return device(blk * 2 + zhi, lax.div(y, 2), z, c)

    def by_row(s):
        return device((x * 2 + s) * 2 + zhi, lax.div(y, 2), z, lax.rem(y, 2))

    core_dev = device(row, x, z, other)
    stays = blk == y

    sent = []
    turned = []

    def send(src, dst, name, n, dev, at=None):
        copy = remote(src, dst, sem[name][0].at[n], sem[name][1].at[n if at is None else at], dev)
        copy.start()
        sent.append(copy)

    def turn(src, dst, name, at, dev):
        away = remote(src, dst, sem[name][0].at[0], sem[name][1].at[at], dev)
        here = pltpu.make_async_copy(src, dst, sem[name][1].at[at])

        @pl.when(stays)
        def _():
            here.start()

        @pl.when(jnp.logical_not(stays))
        def _():
            away.start()

        turned.append(away)

    def arrived(slot, name, n):
        remote(slot, slot, sem[name][0].at[n], sem[name][1].at[n], core_dev).wait_recv()

    loads = [
        pltpu.make_async_copy(src, dst, load_sem.at[n])
        for n, (src, dst) in enumerate((
            (pair_h, pair), (w_query_h, w_query), (w_key_h, w_key), (w_value_h, w_value),
            (w_gate_h, w_gate), (w_out_h, w_out), (out_grad_h, out_grad)))
    ]
    for copy in loads:
        copy.start()

    barrier = pltpu.get_barrier_semaphore()
    partners = (
        [zz_dev(e, d) for e in range(2) for d in range(4) if (e, d) != (0, 0)]
        + [core_dev, x_dev(1), x_dev(3)] + [y_dev(d) for d in (1, 7, 2, 6)]
        + [by_column(other), by_row(other)]
    )

    def greet(dev):
        pl.semaphore_signal(barrier, inc=1, device_id=dev, device_id_type=MESH)

    for dev in partners:
        greet(dev)

    @pl.when(jnp.logical_not(stays))
    def _():
        greet(by_column(core))
        greet(by_row(core))

    gain_v = gain[...]
    for copy in loads:
        copy.wait()

    def norm(values):
        average = jnp.mean(values, axis=-1, keepdims=True)
        centred = values - average
        variance = jnp.mean(centred * centred, axis=-1, keepdims=True)
        rstd = lax.rsqrt(variance + EPS)
        return centred * rstd, rstd, centred

    win = pair[0:8].reshape(256, 128).astype(f32)
    hat, _, _ = norm(win)
    window = (hat * gain_v).astype(bf16)
    query = (nn(window, w_query[...]) * (32 ** (-0.5))).astype(bf16).astype(f32)
    keys = nn(window, w_key[...]).astype(bf16).astype(f32)
    vals = nn(window, w_value[...]).astype(bf16).astype(f32)
    gate = jax.nn.sigmoid(nn(window, w_gate[...])).astype(bf16).astype(f32)
    gg = nt(out_grad[...].reshape(256, 128), w_out[...])
    ga = (gg * gate).astype(bf16).astype(f32)
    gate_s[...] = gate
    gg_s[...] = gg
    for n, array in enumerate((keys, vals, query, ga)):
        for g in range(2):
            outs = lane_swap([array[(g * 4 + b) * 32:(g * 4 + b + 1) * 32] for b in range(4)])
            for h in range(4):
                zsend[h, n, g] = outs[h].astype(bf16)

    pl.semaphore_wait(barrier, len(partners) + jnp.where(stays, 0, 2))

    z_rows = pl.ds(pl.multiple_of(z * 32, 32), 32)
    for d in (1, 3, 2):
        send(zsend.at[z_at(d), 0:2], kv.at[blk, :, :, z_rows, :], "kvz", d, z_dev(d))
    kv[blk, :, :, z_rows, :] = zsend[z, 0:2]
    qd[:, :, z_rows, :] = zsend[z, 2:4]

    pick = lax.broadcasted_iota(jnp.int32, (64, 4), 0) // 16 == lax.broadcasted_iota(
        jnp.int32, (64, 4), 1)
    w_rows[...] = nn(pick.astype(bf16), w_bias[...]).astype(bf16)
    row_in = lax.rem(lax.broadcasted_iota(jnp.int32, (64, 128), 0), 16)

    def tile_step(i, acc):
        for u in range(4):
            jj = i * 4 + u
            tokens = jnp.concatenate([pair[q * 16 + jj] for q in range(4)], axis=0).astype(f32)
            hat, rstd, _ = norm(tokens)
            xhat[jj] = hat
            rstd_all[jj] = jnp.broadcast_to(rstd, (128, 128))
            normed = (hat * gain_v).astype(bf16)
            chosen = jnp.where(row_in == jj, w_rows[...].astype(f32), 0.0).astype(bf16)
            acc = acc + nt(chosen, normed)
        return acc

    tile_bias = lax.fori_loop(0, 4, tile_step, jnp.zeros((64, 128), f32))
    bsend[...] = tile_bias.astype(bf16).reshape(4, 16, 128)
    for e, d in ((0, 1), (0, 3), (0, 2), (1, 0), (1, 1), (1, 3), (1, 2)):
        send(bsend.at[z_at(d)], brecv.at[zhi, z], "bz", e * 4 + d, zz_dev(e, d))
    brecv[zhi, z] = bsend[z]
    for d in (1, 3, 2):
        send(zsend.at[z_at(d), 2:4], qd.at[:, :, z_rows, :], "qdz", d, z_dev(d))

    for d in (1, 2, 3):
        rows_d = pl.ds(pl.multiple_of(z_at(4 - d) * 32, 32), 32)
        arrived(kv.at[blk, :, :, rows_d, :], "kvz", d)
    send(kv.at[blk, 0], kv.at[blk, 0], "kva", 0, x_dev(1))
    send(kv.at[blk, 1], kv.at[blk, 1], "kva", 1, x_dev(3))
    send(kv.at[blk, 1], kv.at[blk, 1], "kva", 2, x_dev(1))
    send(kv.at[blk, 0], kv.at[blk, 0], "kva", 3, x_dev(3))
    send(kv.at[blk], kv.at[blk], "kvc", 0, core_dev)

    for e in range(2):
        for d in range(4):
            if (e, d) != (0, 0):
                arrived(brecv.at[lax.rem(zhi + e, 2), z_at(4 - d)], "bz", e * 4 + d)
    for e in range(2):
        outs = lane_swap([brecv[e, b].astype(f32) for b in range(4)])
        for q in range(4):
            grid[e, q * 16:(q + 1) * 16] = outs[q].astype(bf16)

    def half(c):
        return grid.at[:, pl.ds(pl.multiple_of(c * 32, 32), 32), :]

    turn(half(core), bias.at[blk, lax.rem(y, 2)], "bt", lax.rem(y, 2), by_column(core))
    send(half(other), bias.at[blk, lax.rem(y, 2)], "bt", 1, by_column(other), lax.rem(y, 2))

    k_minus, k_plus, k_two = x_at(3) * 2 + core, x_at(1) * 2 + core, x_at(2) * 2 + core
    arrived(kv.at[k_minus, 0], "kva", 0)
    send(kv.at[k_minus, 0], kv.at[k_minus, 0], "kvb", 0, x_dev(1))
    arrived(kv.at[k_plus, 1], "kva", 1)
    send(kv.at[k_plus, 1], kv.at[k_plus, 1], "kvb", 1, x_dev(3))

    arrived(bias.at[y, 0], "bt", 0)
    arrived(bias.at[y, 1], "bt", 1)
    for d in (2, 6, 1, 7):
        send(bias.at[y], bias.at[y], "ya", d, y_dev(d))

    arrived(kv.at[k_minus, 1], "kva", 2)
    send(kv.at[k_minus], kv.at[k_minus], "kvc", 1, core_dev)
    arrived(kv.at[k_plus, 0], "kva", 3)
    send(kv.at[k_plus], kv.at[k_plus], "kvc", 2, core_dev)

    for d in (1, 2, 3):
        rows_d = pl.ds(pl.multiple_of(z_at(4 - d) * 32, 32), 32)
        arrived(qd.at[:, :, rows_d, :], "qdz", d)
    for n in range(2):
        for g in range(2):
            qdt[n, g] = qd[n, g].astype(f32).T.astype(bf16)

    arrived(bias.at[y_at(6)], "ya", 2)
    send(bias.at[y_at(6)], bias.at[y_at(6)], "ya", 3, y_dev(1))
    send(bias.at[y_at(6), 0], bias.at[y_at(6), 0], "yb", 0, y_dev(2))
    arrived(bias.at[y_at(2)], "ya", 6)
    send(bias.at[y_at(2)], bias.at[y_at(2)], "ya", 5, y_dev(7))
    send(bias.at[y_at(2), 1], bias.at[y_at(2), 1], "yb", 1, y_dev(6))

    arrived(kv.at[k_two, 0], "kvb", 0)
    arrived(kv.at[k_two, 1], "kvb", 1)
    send(kv.at[k_two], kv.at[k_two], "kvc", 3, core_dev)

    arrived(bias.at[y_at(7)], "ya", 1)
    arrived(bias.at[y_at(1)], "ya", 7)
    arrived(bias.at[y_at(5)], "ya", 3)
    arrived(bias.at[y_at(3)], "ya", 5)
    arrived(bias.at[y_at(4), 0], "yb", 0)
    arrived(bias.at[y_at(4), 1], "yb", 1)
    for n, d in enumerate((0, 3, 1, 2)):
        arrived(kv.at[x_at(d) * 2 + other], "kvc", n)

    spot = lax.broadcasted_iota(jnp.int32, (1, 1024), 1)
    spot_c = (lax.div(spot, 256) * 8 + lax.rem(lax.div(spot, 32), 4) * 2
              + lax.rem(lax.div(spot, 128), 2))
    keep = spot_c * 32 + lax.rem(spot, 32) < length[0]
    for b in range(8):
        bias_f[:, b * 128:(b + 1) * 128] = bias[b].reshape(128, 128).astype(f32)
    dbias[...] = jnp.zeros_like(dbias)
    att[...] = jnp.zeros_like(att)
    dqkv[0] = jnp.zeros_like(dqkv[0])
    lanes = lane_block((128, 128))

    def cores_summed(g):
        arrived(dkv_c.at[g], "dkvc", g)
        for b in range(4):
            dkv_m[g, b] = (dkv_send[core, g, b].astype(f32) + dkv_c[g, b].astype(f32)).astype(bf16)
        send(dkv_m.at[g, x_at(2), 0], dkv_r.at[g, 0], "dr", g * 2, x_dev(1))
        send(dkv_m.at[g, x_at(2), 1], dkv_r.at[g, 1], "dr", g * 2 + 1, x_dev(3))
        send(dkv_m.at[g, x_at(1), 1], dkv_in.at[g, 0, 1], "df", g * 4, x_dev(1))
        send(dkv_m.at[g, x_at(3), 0], dkv_in.at[g, 1, 0], "df", g * 4 + 1, x_dev(3))

    for g in range(2):
        def attend(a, carry):
            own = lanes == a
            key = kv[:, 0, g].reshape(1024, 128)
            value = kv[:, 1, g].reshape(1024, 128)
            q_a = jnp.where(own, qd[0, g].astype(f32), 0.0).astype(bf16)
            do_f = jnp.where(own, qd[1, g].astype(f32), 0.0)
            do_a = do_f.astype(bf16)
            logits = jnp.where(keep, nt(q_a, key) + bias_f[...], NEG)
            top = jnp.max(logits, axis=-1, keepdims=True)
            expo = jnp.exp(logits - top)
            inv = 1.0 / jnp.sum(expo, axis=-1, keepdims=True)
            out = nn(expo.astype(bf16), value) * inv
            out = jnp.where(own, out, 0.0)
            att[g] = att[g] + out
            delta = jnp.sum(do_f * out, axis=-1, keepdims=True)
            shares = expo * inv
            grads = shares * (nt(do_a, value) - delta)
            for b in range(8):
                dbias[b] = dbias[b] + grads[:, b * 128:(b + 1) * 128]
            grads_b = grads.astype(bf16)
            dq = nn(grads_b, key) * (32 ** (-0.5))
            dqkv[0, g] = jnp.where(own, dq, dqkv[0, g].astype(f32)).astype(bf16)
            part = pl.ds(pl.multiple_of(a * 32, 32), 32)
            dk = nn(qdt[0, g, part, :], grads_b).astype(bf16)
            dv = nn(qdt[1, g, part, :], shares.astype(bf16)).astype(bf16)
            for b in range(8):
                dkv_send[b % 2, g, b // 2, 0, part, :] = dk[:, b * 128:(b + 1) * 128]
                dkv_send[b % 2, g, b // 2, 1, part, :] = dv[:, b * 128:(b + 1) * 128]
            return carry

        lax.fori_loop(0, 2, attend, 0)
        if g == 1:
            cores_summed(0)
        lax.fori_loop(2, 4, attend, 0)
        send(dkv_send.at[other, g], dkv_c.at[g], "dkvc", g, core_dev)

    for b in range(8):
        db_send[b] = dbias[b].astype(bf16)
    send(db_send.at[y_at(3)], db_r.at[0], "yr", 0, y_dev(1))
    send(db_send.at[y_at(5)], db_r.at[1], "yr", 1, y_dev(7))
    send(db_send.at[y_at(4), 0:64], db_rh.at[0], "yr", 2, y_dev(2))
    send(db_send.at[y_at(4), 64:128], db_rh.at[1], "yr", 3, y_dev(6))
    send(db_send.at[y_at(1)], db_y.at[0], "yd", 0, y_dev(1))
    send(db_send.at[y_at(7)], db_y.at[1], "yd", 1, y_dev(7))
    for d in (1, 3, 2):
        rows_d = pl.ds(pl.multiple_of(z_at(d) * 32, 32), 32)
        send(att.at[:, rows_d, :], o_in.at[z], "oz", d, z_dev(d))
        send(dqkv.at[0, :, rows_d, :], e_in.at[z, 0], "dqz", d, z_dev(d))
    o_in[z] = att[:, z_rows, :]
    e_in[z, 0] = dqkv[0, :, z_rows, :]

    cores_summed(1)

    arrived(db_r.at[0], "yr", 0)
    arrived(db_rh.at[0], "yr", 2)
    near = dbias[y_at(2)] + db_r[0].astype(f32)
    db_2[0, 0:64] = (near[0:64] + db_rh[0].astype(f32)).astype(bf16)
    db_2[0, 64:128] = near[64:128].astype(bf16)
    send(db_2.at[0], db_y.at[2], "yd", 2, y_dev(2))
    arrived(db_r.at[1], "yr", 1)
    arrived(db_rh.at[1], "yr", 3)
    near = dbias[y_at(6)] + db_r[1].astype(f32)
    db_2[1, 0:64] = near[0:64].astype(bf16)
    db_2[1, 64:128] = (near[64:128] + db_rh[1].astype(f32)).astype(bf16)
    send(db_2.at[1], db_y.at[3], "yd", 3, y_dev(6))

    for g in range(2):
        arrived(dkv_r.at[g, 0], "dr", g * 2)
        dkv_2[g, 0] = (dkv_m[g, x_at(1), 0].astype(f32) + dkv_r[g, 0].astype(f32)).astype(bf16)
        send(dkv_2.at[g, 0], dkv_in.at[g, 0, 0], "df", g * 4 + 2, x_dev(1))
        arrived(dkv_r.at[g, 1], "dr", g * 2 + 1)
        dkv_2[g, 1] = (dkv_m[g, x_at(3), 1].astype(f32) + dkv_r[g, 1].astype(f32)).astype(bf16)
        send(dkv_2.at[g, 1], dkv_in.at[g, 1, 1], "df", g * 4 + 3, x_dev(3))

    total = dbias[y]
    for n in range(4):
        arrived(db_y.at[n], "yd", n)
        total = total + db_y[n].astype(f32)
    db_s[...] = total.reshape(2, 64, 128)
    turn(db_s.at[core], db_t.at[core], "dt", core, by_row(core))
    send(db_s.at[other], db_t.at[core], "dt", 1, by_row(other), core)

    for g in range(2):
        arrived(dkv_in.at[g, 0, 1], "df", g * 4)
        arrived(dkv_in.at[g, 1, 0], "df", g * 4 + 1)
        arrived(dkv_in.at[g, 0, 0], "df", g * 4 + 2)
        arrived(dkv_in.at[g, 1, 1], "df", g * 4 + 3)
        for n in range(2):
            total = dkv_m[g, x, n].astype(f32) + (
                dkv_in[g, 0, n].astype(f32) + dkv_in[g, 1, n].astype(f32))
            dqkv[1 + n, g] = total.T.astype(bf16)
    for d in (1, 3, 2):
        rows_d = pl.ds(pl.multiple_of(z_at(d) * 32, 32), 32)
        send(dqkv.at[1:3, :, rows_d, :], e_in.at[z, 1:3], "dkvz", d, z_dev(d))
    e_in[z, 1:3] = dqkv[1:3, :, z_rows, :]

    arrived(db_t.at[0], "dt", 0)
    arrived(db_t.at[1], "dt", 1)
    for e in range(2):
        final = db_t[:, e * 32:(e + 1) * 32, :].reshape(64, 128)
        outs = lane_swap([final[q * 16:(q + 1) * 16] for q in range(4)])
        for b in range(4):
            db_out[e, b] = outs[b]
    for e, d in ((0, 1), (0, 3), (0, 2), (1, 0), (1, 1), (1, 3), (1, 2)):
        send(db_out.at[lax.rem(zhi + e, 2), z_at(d)], db_in.at[zhi, z], "dbz", e * 4 + d,
             zz_dev(e, d))
    db_in[zhi, z] = db_out[zhi, z]

    for d in (1, 2, 3):
        h_d = z_at(4 - d)
        arrived(o_in.at[h_d], "oz", d)
        arrived(e_in.at[h_d, 0], "dqz", d)
    gated = []
    pres = []
    for g in range(2):
        outs = lane_swap([o_in[h, g] for h in range(4)])
        for i in range(4):
            at = slice((g * 4 + i) * 32, (g * 4 + i + 1) * 32)
            gate_t, gg_t = gate_s[at], gg_s[at]
            gated.append((gate_t * outs[i]).astype(bf16))
            pres.append((gg_t * outs[i] * gate_t * (1.0 - gate_t)).astype(bf16))
    update[...] = nn(jnp.concatenate(gated, axis=0), w_out[...]).astype(bf16).reshape(8, 32, 128)
    for d in (1, 2, 3):
        arrived(e_in.at[z_at(4 - d), 1:3], "dkvz", d)
    sides = [jnp.concatenate(pres, axis=0)]
    for n in range(3):
        tiles = []
        for g in range(2):
            tiles += lane_swap([e_in[h, n, g].astype(f32) for h in range(4)])
        sides.append(jnp.concatenate(tiles, axis=0).astype(bf16))
    grad_window = (nt(sides[1], w_query[...]) + nt(sides[2], w_key[...])
                   + nt(sides[3], w_value[...]) + nt(sides[0], w_gate[...]))
    gw[0:8] = grad_window.reshape(8, 32, 128)
    gw[8:16] = jnp.zeros((8, 32, 128), f32)

    for e in range(2):
        for d in range(4):
            if (e, d) != (0, 0):
                arrived(db_in.at[lax.rem(zhi + e, 2), z_at(4 - d)], "dbz", e * 4 + d)
    flat = (db_in[0] + db_in[1]).reshape(64, 128).T
    high = flat.astype(bf16)
    rest = flat - high.astype(f32)
    mid = rest.astype(bf16)
    low = (rest - mid.astype(f32)).astype(bf16)

    def final_step(i, carry):
        for u in range(2):
            jj = i * 2 + u
            chosen = jnp.where(row_in == jj, w_rows[...].astype(f32), 0.0).astype(bf16)
            grad = nn(high, chosen) + (nn(mid, chosen) + nn(low, chosen))
            grad = jnp.concatenate([grad[0:32] + gw[jj], grad[32:]], axis=0) * gain_v
            hat = xhat[jj]
            first = jnp.mean(grad, axis=-1, keepdims=True)
            second = jnp.mean(grad * hat, axis=-1, keepdims=True)
            result = rstd_all[jj] * (grad - first - hat * second)
            for q in range(4):
                pair_grad[q * 16 + jj] = result[q * 32:(q + 1) * 32]
        return carry

    lax.fori_loop(0, 8, final_step, 0)

    for copy in sent:
        copy.wait_send()

    @pl.when(jnp.logical_not(stays))
    def _():
        for copy in turned:
            copy.wait_send()


def body(pair, length, ln_gain, w_query, w_key, w_value, w_gate, w_bias, w_out, out_grad):
    vmem = pl.BlockSpec(memory_space=pltpu.VMEM)
    hbm = pl.BlockSpec(memory_space=pltpu.HBM)
    smem = pl.BlockSpec(memory_space=pltpu.SMEM)

    scratch = [
        pltpu.VMEM(pair.shape, bf16),
        *[pltpu.VMEM((128, 128), bf16) for _ in range(5)],
        pltpu.VMEM(out_grad.shape, bf16),
        pltpu.SemaphoreType.DMA((7,)),
        pltpu.VMEM((16, 128, 128), f32),
        pltpu.VMEM((16, 128, 128), f32),
        pltpu.VMEM((64, 128), bf16),
        pltpu.VMEM((256, 128), f32),
        pltpu.VMEM((256, 128), f32),
        pltpu.VMEM((4, 4, 2, 32, 128), bf16),
        pltpu.VMEM((8, 2, 2, 128, 128), bf16),
        pltpu.VMEM((2, 2, 128, 128), bf16),
        pltpu.VMEM((2, 2, 128, 128), bf16),
        pltpu.VMEM((4, 16, 128), bf16),
        pltpu.VMEM((2, 4, 16, 128), bf16),
        pltpu.VMEM((2, 64, 128), bf16),
        pltpu.VMEM((8, 2, 2, 32, 128), bf16),
        pltpu.VMEM((128, 1024), f32),
        pltpu.VMEM((8, 128, 128), f32),
        pltpu.VMEM((2, 128, 128), f32),
        pltpu.VMEM((3, 2, 128, 128), bf16),
        pltpu.VMEM((8, 128, 128), bf16),
        pltpu.VMEM((2, 128, 128), bf16),
        pltpu.VMEM((2, 64, 128), bf16),
        pltpu.VMEM((2, 128, 128), bf16),
        pltpu.VMEM((4, 128, 128), bf16),
        pltpu.VMEM((2, 64, 128), f32),
        pltpu.VMEM((2, 64, 128), f32),
        pltpu.VMEM((2, 4, 16, 128), f32),
        pltpu.VMEM((2, 4, 16, 128), f32),
        pltpu.VMEM((2, 2, 4, 2, 128, 128), bf16),
        pltpu.VMEM((2, 4, 2, 128, 128), bf16),
        pltpu.VMEM((2, 4, 2, 128, 128), bf16),
        pltpu.VMEM((2, 2, 128, 128), bf16),
        pltpu.VMEM((2, 2, 128, 128), bf16),
        pltpu.VMEM((2, 2, 2, 128, 128), bf16),
        pltpu.VMEM((4, 3, 2, 32, 128), bf16),
        pltpu.VMEM((4, 2, 32, 128), f32),
        pltpu.VMEM((16, 32, 128), f32),
    ]
    for _, n in COPIES:
        scratch += [pltpu.SemaphoreType.DMA((n,)), pltpu.SemaphoreType.DMA((n,))]
    call = pl.pallas_call(
        kernel,
        out_shape=(
            jax.ShapeDtypeStruct(out_grad.shape, bf16),
            jax.ShapeDtypeStruct(pair.shape, f32),
        ),
        in_specs=[hbm, smem, vmem, hbm, hbm, hbm, hbm, vmem, hbm, hbm],
        out_specs=(vmem, vmem),
        scratch_shapes=scratch,
        compiler_params=pltpu.CompilerParams(
            collective_id=0, has_side_effects=True, vmem_limit_bytes=63 * 1024 * 1024
        ),
    )
    return call(
        pair, length, ln_gain.reshape(1, 128), w_query, w_key, w_value, w_gate, w_bias.T, w_out,
        out_grad,
    )


def solution(mesh):
    tiled = P("rows", "cols", None)
    placed = (tiled, P(), P(), P(), P(), P(), P(), P(), P(), tiled)
    return jax.shard_map(
        body, mesh=mesh, in_specs=placed, out_specs=(tiled, tiled), check_vma=False
    )
```

time: 79.4 us -> 71.8 us (0.904)
  the two profiles are of different devices: /device:TPU:1 before, /device:TPU:4 now
where the time goes in v2:
time: 71.8 us; the launch traced here: 71.6 us
  Pallas kernels  66.6 us (93%)
  local copies, waits for them, and re-layouts  3.74 us (5%)
  between operations  1.29 us (2%)
    pallas_call x1, Pallas kernels, body(): call(pair, length, ln_gain.reshape(1, 128), w_query, w_key, w_value, w_ga...  66.6 us
    unnamed x2, local copies, waits for them, and re-layouts  3.74 us

profile of v2, /device:TPU:4, one launch (start us, length us, event | category | flops | bytes accessed | tf_op | source)
XLA Modules:
  0.0 71.6 jit_solution(3628930522676891613)
XLA Ops:
  1.3 66.6 %shard_map.113 = (bf16[8,32,128]{2,1,0:T(8,128)(2,1)}, f32[64,32,128]{2,1,0:T(8,128)}) custom-call(bf16[64,32,128]{2,1,0:T(8,128)(2,1)} %pair_h.1, s32[1]{0:T(128)S(6)} %copy.14.length, f32[1,128]{1,0:T(1,128)} %bitcast.3, bf16[128,128]{1,0:T(8,128)(2,1)} %w_query_h.1, bf16[128,128]{1,0:T(8,128)(2,1)} %w_key_h.1, bf16[128,128]{1,0:T(8,128)(2,1)} %w_value_h.1, ...), custom_call_target="tpu_custom_call" | custom-call | tf_op jit(solution)/shard_map/pallas_call | solution.py:534
  67.8 1.5 %copy.15 = bf16[8,32,128]{2,1,0:T(8,128)(2,1)} copy(bf16[8,32,128]{2,1,0:T(8,128)(2,1)} %get-tuple-element.4) | data formatting | bytes 131072
  69.3 2.3 %copy.16 = f32[64,32,128]{2,1,0:T(8,128)} copy(f32[64,32,128]{2,1,0:T(8,128)} %get-tuple-element.5) | data formatting | bytes 2097152

commit v3 on v2

--- a/solution.py
+++ b/solution.py
@@ -11,10 +11,11 @@
 f32 = jnp.float32
 bf16 = jnp.bfloat16
 COPIES = (
-    ("kvz", 4), ("qdz", 4), ("bz", 8), ("kva", 4), ("kvb", 2), ("kvc", 4), ("bt", 2), ("ya", 8),
-    ("yb", 2), ("dkvc", 2), ("dr", 4), ("df", 8), ("yr", 4), ("yd", 4), ("dt", 2), ("dbz", 8),
-    ("oz", 4), ("dqz", 4), ("dkvz", 4),
+    ("kvz", 4), ("qdz", 4), ("bt", 16), ("kvx", 4), ("kvc", 4), ("ya", 8), ("dkvc", 2), ("dr", 8),
+    ("yr", 8), ("dt", 16), ("oz", 4), ("dqz", 4), ("dkvz", 4),
 )
+
+AROUND = ((0, 0), (0, 1), (0, 3), (0, 2), (1, 0), (1, 1), (1, 3), (1, 2))
 
 
 def nn(left, right):
@@ -52,9 +53,8 @@
 def kernel(
     pair_h, length, gain, w_query_h, w_key_h, w_value_h, w_gate_h, w_bias, w_out_h, out_grad_h,
     update, pair_grad,
-    pair, w_query, w_key, w_value, w_gate, w_out, out_grad, load_sem, xhat, rstd_all, w_rows, gate_s, gg_s, zsend, kv, qd, qdt, bsend, brecv, grid, bias, bias_f,
-    dbias, att, dqkv, db_send, db_r, db_rh, db_2, db_y, db_s, db_t, db_out, db_in,
-    dkv_send, dkv_c, dkv_m, dkv_r, dkv_2, dkv_in,
+    pair, w_query, w_key, w_value, w_gate, w_out, out_grad, load_sem, xhat, rstd_all, w_rows, gate_s, gg_s, zsend, kv, qd, qdt, bsend, brecv, bias, bias_f,
+    dbias, att, dqkv, db_send, db_y, db_out, db_in, dkv_send, dkv_c, dkv_m, dkv_in,
     e_in, o_in, gw,
     *sems,
 ):
@@ -75,9 +75,6 @@
     def z_dev(d):
         return device(row, x, z_at(d), core)
 
-    def zz_dev(e, d):
-        return device(y * 2 + lax.rem(zhi + e, 2), x, z_at(d), core)
-
     def x_at(d):
         return lax.rem(x + d, 4)
 
@@ -90,11 +87,12 @@
     def y_dev(d):
         return device(y_at(d) * 2 + zhi, x, z, core)
 
-    def by_column(c):
-        return device(blk * 2 + zhi, lax.div(y, 2), z, c)
-
-    def by_row(s):
-        return device((x * 2 + s) * 2 + zhi, lax.div(y, 2), z, lax.rem(y, 2))
+    def by_column(e, d, c):
+        return device(blk * 2 + lax.rem(zhi + e, 2), lax.div(y, 2), z_at(d), c)
+
+    def by_row(e, d, s):
+        return device(
+            (x * 2 + s) * 2 + lax.rem(zhi + e, 2), lax.div(y, 2), z_at(d), lax.rem(y, 2))
 
     core_dev = device(row, x, z, other)
     stays = blk == y
@@ -107,7 +105,7 @@
         copy.start()
         sent.append(copy)
 
-    def turn(src, dst, name, at, dev):
+    def turn_own(src, dst, name, at, dev):
         away = remote(src, dst, sem[name][0].at[0], sem[name][1].at[at], dev)
         here = pltpu.make_async_copy(src, dst, sem[name][1].at[at])
 
@@ -134,11 +132,11 @@
         copy.start()
 
     barrier = pltpu.get_barrier_semaphore()
-    partners = (
-        [zz_dev(e, d) for e in range(2) for d in range(4) if (e, d) != (0, 0)]
-        + [core_dev, x_dev(1), x_dev(3)] + [y_dev(d) for d in (1, 7, 2, 6)]
-        + [by_column(other), by_row(other)]
-    )
+    turns = [(e, d, other) for e in range(2) for d in range(4)]
+    turns += [(e, d, core) for e in range(2) for d in range(4) if (e, d) != (0, 0)]
+    partners = [z_dev(d) for d in (1, 2, 3)] + [core_dev] + [x_dev(d) for d in (1, 2, 3)]
+    partners += [y_dev(d) for d in range(1, 8)]
+    partners += [by_column(*turn) for turn in turns] + [by_row(*turn) for turn in turns]
 
     def greet(dev):
         pl.semaphore_signal(barrier, inc=1, device_id=dev, device_id_type=MESH)
@@ -148,8 +146,8 @@
 
     @pl.when(jnp.logical_not(stays))
     def _():
-        greet(by_column(core))
-        greet(by_row(core))
+        greet(by_column(0, 0, core))
+        greet(by_row(0, 0, core))
 
     gain_v = gain[...]
     for copy in loads:
@@ -206,51 +204,33 @@
 
     tile_bias = lax.fori_loop(0, 4, tile_step, jnp.zeros((64, 128), f32))
     bsend[...] = tile_bias.astype(bf16).reshape(4, 16, 128)
-    for e, d in ((0, 1), (0, 3), (0, 2), (1, 0), (1, 1), (1, 3), (1, 2)):
-        send(bsend.at[z_at(d)], brecv.at[zhi, z], "bz", e * 4 + d, zz_dev(e, d))
-    brecv[zhi, z] = bsend[z]
+    odd = lax.rem(y, 2)
+    turn_own(bsend.at[z], brecv.at[odd, zhi, z], "bt", odd * 8, by_column(0, 0, core))
+    for n, c in enumerate((core, other)):
+        for e, d in AROUND:
+            if (n, e, d) != (0, 0, 0):
+                send(bsend.at[z_at(d)], brecv.at[odd, zhi, z], "bt", n * 8 + e * 4 + d,
+                     by_column(e, d, c), odd * 8 + e * 4 + d)
     for d in (1, 3, 2):
         send(zsend.at[z_at(d), 2:4], qd.at[:, :, z_rows, :], "qdz", d, z_dev(d))
 
     for d in (1, 2, 3):
         rows_d = pl.ds(pl.multiple_of(z_at(4 - d) * 32, 32), 32)
         arrived(kv.at[blk, :, :, rows_d, :], "kvz", d)
-    send(kv.at[blk, 0], kv.at[blk, 0], "kva", 0, x_dev(1))
-    send(kv.at[blk, 1], kv.at[blk, 1], "kva", 1, x_dev(3))
-    send(kv.at[blk, 1], kv.at[blk, 1], "kva", 2, x_dev(1))
-    send(kv.at[blk, 0], kv.at[blk, 0], "kva", 3, x_dev(3))
+    for d in (1, 3, 2):
+        send(kv.at[blk], kv.at[blk], "kvx", d, x_dev(d))
     send(kv.at[blk], kv.at[blk], "kvc", 0, core_dev)
 
-    for e in range(2):
-        for d in range(4):
-            if (e, d) != (0, 0):
-                arrived(brecv.at[lax.rem(zhi + e, 2), z_at(4 - d)], "bz", e * 4 + d)
-    for e in range(2):
-        outs = lane_swap([brecv[e, b].astype(f32) for b in range(4)])
-        for q in range(4):
-            grid[e, q * 16:(q + 1) * 16] = outs[q].astype(bf16)
-
-    def half(c):
-        return grid.at[:, pl.ds(pl.multiple_of(c * 32, 32), 32), :]
-
-    turn(half(core), bias.at[blk, lax.rem(y, 2)], "bt", lax.rem(y, 2), by_column(core))
-    send(half(other), bias.at[blk, lax.rem(y, 2)], "bt", 1, by_column(other), lax.rem(y, 2))
-
-    k_minus, k_plus, k_two = x_at(3) * 2 + core, x_at(1) * 2 + core, x_at(2) * 2 + core
-    arrived(kv.at[k_minus, 0], "kva", 0)
-    send(kv.at[k_minus, 0], kv.at[k_minus, 0], "kvb", 0, x_dev(1))
-    arrived(kv.at[k_plus, 1], "kva", 1)
-    send(kv.at[k_plus, 1], kv.at[k_plus, 1], "kvb", 1, x_dev(3))
-
-    arrived(bias.at[y, 0], "bt", 0)
-    arrived(bias.at[y, 1], "bt", 1)
-    for d in (2, 6, 1, 7):
+    for n in range(2):
+        for e, d in AROUND:
+            arrived(brecv.at[n, lax.rem(zhi + e, 2), z_at(4 - d)], "bt", n * 8 + e * 4 + d)
+    for n in range(2):
+        for e in range(2):
+            outs = lane_swap([brecv[n, e, b].astype(f32) for b in range(4)])
+            bias[y, n, e, 0:16] = jnp.where(core == 0, outs[0], outs[2]).astype(bf16)
+            bias[y, n, e, 16:32] = jnp.where(core == 0, outs[1], outs[3]).astype(bf16)
+    for d in (4, 3, 5, 2, 6, 1, 7):
         send(bias.at[y], bias.at[y], "ya", d, y_dev(d))
-
-    arrived(kv.at[k_minus, 1], "kva", 2)
-    send(kv.at[k_minus], kv.at[k_minus], "kvc", 1, core_dev)
-    arrived(kv.at[k_plus, 0], "kva", 3)
-    send(kv.at[k_plus], kv.at[k_plus], "kvc", 2, core_dev)
 
     for d in (1, 2, 3):
         rows_d = pl.ds(pl.multiple_of(z_at(4 - d) * 32, 32), 32)
@@ -259,25 +239,15 @@
         for g in range(2):
             qdt[n, g] = qd[n, g].astype(f32).T.astype(bf16)
 
-    arrived(bias.at[y_at(6)], "ya", 2)
-    send(bias.at[y_at(6)], bias.at[y_at(6)], "ya", 3, y_dev(1))
-    send(bias.at[y_at(6), 0], bias.at[y_at(6), 0], "yb", 0, y_dev(2))
-    arrived(bias.at[y_at(2)], "ya", 6)
-    send(bias.at[y_at(2)], bias.at[y_at(2)], "ya", 5, y_dev(7))
-    send(bias.at[y_at(2), 1], bias.at[y_at(2), 1], "yb", 1, y_dev(6))
-
-    arrived(kv.at[k_two, 0], "kvb", 0)
-    arrived(kv.at[k_two, 1], "kvb", 1)
-    send(kv.at[k_two], kv.at[k_two], "kvc", 3, core_dev)
-
-    arrived(bias.at[y_at(7)], "ya", 1)
-    arrived(bias.at[y_at(1)], "ya", 7)
-    arrived(bias.at[y_at(5)], "ya", 3)
-    arrived(bias.at[y_at(3)], "ya", 5)
-    arrived(bias.at[y_at(4), 0], "yb", 0)
-    arrived(bias.at[y_at(4), 1], "yb", 1)
-    for n, d in enumerate((0, 3, 1, 2)):
-        arrived(kv.at[x_at(d) * 2 + other], "kvc", n)
+    for d in (1, 3, 2):
+        k_d = x_at(4 - d) * 2 + core
+        arrived(kv.at[k_d], "kvx", d)
+        send(kv.at[k_d], kv.at[k_d], "kvc", d, core_dev)
+    for d in (0, 1, 3, 2):
+        arrived(kv.at[x_at(4 - d) * 2 + other], "kvc", d)
+
+    for d in range(1, 8):
+        arrived(bias.at[y_at(8 - d)], "ya", d)
 
     spot = lax.broadcasted_iota(jnp.int32, (1, 1024), 1)
     spot_c = (lax.div(spot, 256) * 8 + lax.rem(lax.div(spot, 32), 4) * 2
@@ -294,10 +264,8 @@
         arrived(dkv_c.at[g], "dkvc", g)
         for b in range(4):
             dkv_m[g, b] = (dkv_send[core, g, b].astype(f32) + dkv_c[g, b].astype(f32)).astype(bf16)
-        send(dkv_m.at[g, x_at(2), 0], dkv_r.at[g, 0], "dr", g * 2, x_dev(1))
-        send(dkv_m.at[g, x_at(2), 1], dkv_r.at[g, 1], "dr", g * 2 + 1, x_dev(3))
-        send(dkv_m.at[g, x_at(1), 1], dkv_in.at[g, 0, 1], "df", g * 4, x_dev(1))
-        send(dkv_m.at[g, x_at(3), 0], dkv_in.at[g, 1, 0], "df", g * 4 + 1, x_dev(3))
+        for d in (1, 3, 2):
+            send(dkv_m.at[g, x_at(d)], dkv_in.at[g, d], "dr", g * 4 + d, x_dev(d))
 
     for g in range(2):
         def attend(a, carry):
@@ -338,12 +306,8 @@
 
     for b in range(8):
         db_send[b] = dbias[b].astype(bf16)
-    send(db_send.at[y_at(3)], db_r.at[0], "yr", 0, y_dev(1))
-    send(db_send.at[y_at(5)], db_r.at[1], "yr", 1, y_dev(7))
-    send(db_send.at[y_at(4), 0:64], db_rh.at[0], "yr", 2, y_dev(2))
-    send(db_send.at[y_at(4), 64:128], db_rh.at[1], "yr", 3, y_dev(6))
-    send(db_send.at[y_at(1)], db_y.at[0], "yd", 0, y_dev(1))
-    send(db_send.at[y_at(7)], db_y.at[1], "yd", 1, y_dev(7))
+    for d in (4, 3, 5, 2, 6, 1, 7):
+        send(db_send.at[y_at(d)], db_y.at[d], "yr", d, y_dev(d))
     for d in (1, 3, 2):
         rows_d = pl.ds(pl.multiple_of(z_at(d) * 32, 32), 32)
         send(att.at[:, rows_d, :], o_in.at[z], "oz", d, z_dev(d))
@@ -353,60 +317,36 @@
 
     cores_summed(1)
 
-    arrived(db_r.at[0], "yr", 0)
-    arrived(db_rh.at[0], "yr", 2)
-    near = dbias[y_at(2)] + db_r[0].astype(f32)
-    db_2[0, 0:64] = (near[0:64] + db_rh[0].astype(f32)).astype(bf16)
-    db_2[0, 64:128] = near[64:128].astype(bf16)
-    send(db_2.at[0], db_y.at[2], "yd", 2, y_dev(2))
-    arrived(db_r.at[1], "yr", 1)
-    arrived(db_rh.at[1], "yr", 3)
-    near = dbias[y_at(6)] + db_r[1].astype(f32)
-    db_2[1, 0:64] = near[0:64].astype(bf16)
-    db_2[1, 64:128] = (near[64:128] + db_rh[1].astype(f32)).astype(bf16)
-    send(db_2.at[1], db_y.at[3], "yd", 3, y_dev(6))
+    total = dbias[y]
+    for d in range(1, 8):
+        arrived(db_y.at[d], "yr", d)
+        total = total + db_y[d].astype(f32)
+    total = total.reshape(2, 2, 2, 16, 128)
+    for n in range(2):
+        for e in range(2):
+            tiles = [jnp.where(core == c, total[n, e, i], 0.0) for c in range(2) for i in range(2)]
+            outs = lane_swap(tiles)
+            for b in range(4):
+                db_out[n, e, b] = outs[b]
+    turn_own(db_out.at[core, zhi, z], db_in.at[core, zhi, z], "dt", core * 8, by_row(0, 0, core))
+    for n, c in enumerate((core, other)):
+        for e, d in AROUND:
+            if (n, e, d) != (0, 0, 0):
+                send(db_out.at[c, lax.rem(zhi + e, 2), z_at(d)], db_in.at[core, zhi, z], "dt",
+                     n * 8 + e * 4 + d, by_row(e, d, c), core * 8 + e * 4 + d)
 
     for g in range(2):
-        arrived(dkv_r.at[g, 0], "dr", g * 2)
-        dkv_2[g, 0] = (dkv_m[g, x_at(1), 0].astype(f32) + dkv_r[g, 0].astype(f32)).astype(bf16)
-        send(dkv_2.at[g, 0], dkv_in.at[g, 0, 0], "df", g * 4 + 2, x_dev(1))
-        arrived(dkv_r.at[g, 1], "dr", g * 2 + 1)
-        dkv_2[g, 1] = (dkv_m[g, x_at(3), 1].astype(f32) + dkv_r[g, 1].astype(f32)).astype(bf16)
-        send(dkv_2.at[g, 1], dkv_in.at[g, 1, 1], "df", g * 4 + 3, x_dev(3))
-
-    total = dbias[y]
-    for n in range(4):
-        arrived(db_y.at[n], "yd", n)
-        total = total + db_y[n].astype(f32)
-    db_s[...] = total.reshape(2, 64, 128)
-    turn(db_s.at[core], db_t.at[core], "dt", core, by_row(core))
-    send(db_s.at[other], db_t.at[core], "dt", 1, by_row(other), core)
-
-    for g in range(2):
-        arrived(dkv_in.at[g, 0, 1], "df", g * 4)
-        arrived(dkv_in.at[g, 1, 0], "df", g * 4 + 1)
-        arrived(dkv_in.at[g, 0, 0], "df", g * 4 + 2)
-        arrived(dkv_in.at[g, 1, 1], "df", g * 4 + 3)
+        for d in (1, 3, 2):
+            arrived(dkv_in.at[g, d], "dr", g * 4 + d)
         for n in range(2):
-            total = dkv_m[g, x, n].astype(f32) + (
-                dkv_in[g, 0, n].astype(f32) + dkv_in[g, 1, n].astype(f32))
+            total = dkv_m[g, x, n].astype(f32)
+            for d in (1, 2, 3):
+                total = total + dkv_in[g, d, n].astype(f32)
             dqkv[1 + n, g] = total.T.astype(bf16)
     for d in (1, 3, 2):
         rows_d = pl.ds(pl.multiple_of(z_at(d) * 32, 32), 32)
         send(dqkv.at[1:3, :, rows_d, :], e_in.at[z, 1:3], "dkvz", d, z_dev(d))
     e_in[z, 1:3] = dqkv[1:3, :, z_rows, :]
-
-    arrived(db_t.at[0], "dt", 0)
-    arrived(db_t.at[1], "dt", 1)
-    for e in range(2):
-        final = db_t[:, e * 32:(e + 1) * 32, :].reshape(64, 128)
-        outs = lane_swap([final[q * 16:(q + 1) * 16] for q in range(4)])
-        for b in range(4):
-            db_out[e, b] = outs[b]
-    for e, d in ((0, 1), (0, 3), (0, 2), (1, 0), (1, 1), (1, 3), (1, 2)):
-        send(db_out.at[lax.rem(zhi + e, 2), z_at(d)], db_in.at[zhi, z], "dbz", e * 4 + d,
-             zz_dev(e, d))
-    db_in[zhi, z] = db_out[zhi, z]
 
     for d in (1, 2, 3):
         h_d = z_at(4 - d)
@@ -435,11 +375,10 @@
     gw[0:8] = grad_window.reshape(8, 32, 128)
     gw[8:16] = jnp.zeros((8, 32, 128), f32)
 
-    for e in range(2):
-        for d in range(4):
-            if (e, d) != (0, 0):
-                arrived(db_in.at[lax.rem(zhi + e, 2), z_at(4 - d)], "dbz", e * 4 + d)
-    flat = (db_in[0] + db_in[1]).reshape(64, 128).T
+    for n in range(2):
+        for e, d in AROUND:
+            arrived(db_in.at[n, lax.rem(zhi + e, 2), z_at(4 - d)], "dt", n * 8 + e * 4 + d)
+    flat = ((db_in[0, 0] + db_in[0, 1]) + (db_in[1, 0] + db_in[1, 1])).reshape(64, 128).T
     high = flat.astype(bf16)
     rest = flat - high.astype(f32)
     mid = rest.astype(bf16)
@@ -490,28 +429,20 @@
         pltpu.VMEM((2, 2, 128, 128), bf16),
         pltpu.VMEM((2, 2, 128, 128), bf16),
         pltpu.VMEM((4, 16, 128), bf16),
-        pltpu.VMEM((2, 4, 16, 128), bf16),
-        pltpu.VMEM((2, 64, 128), bf16),
+        pltpu.VMEM((2, 2, 4, 16, 128), bf16),
         pltpu.VMEM((8, 2, 2, 32, 128), bf16),
         pltpu.VMEM((128, 1024), f32),
         pltpu.VMEM((8, 128, 128), f32),
         pltpu.VMEM((2, 128, 128), f32),
         pltpu.VMEM((3, 2, 128, 128), bf16),
         pltpu.VMEM((8, 128, 128), bf16),
-        pltpu.VMEM((2, 128, 128), bf16),
-        pltpu.VMEM((2, 64, 128), bf16),
-        pltpu.VMEM((2, 128, 128), bf16),
-        pltpu.VMEM((4, 128, 128), bf16),
-        pltpu.VMEM((2, 64, 128), f32),
-        pltpu.VMEM((2, 64, 128), f32),
-        pltpu.VMEM((2, 4, 16, 128), f32),
-        pltpu.VMEM((2, 4, 16, 128), f32),
+        pltpu.VMEM((8, 128, 128), bf16),
+        pltpu.VMEM((2, 2, 4, 16, 128), f32),
+        pltpu.VMEM((2, 2, 4, 16, 128), f32),
         pltpu.VMEM((2, 2, 4, 2, 128, 128), bf16),
         pltpu.VMEM((2, 4, 2, 128, 128), bf16),
         pltpu.VMEM((2, 4, 2, 128, 128), bf16),
-        pltpu.VMEM((2, 2, 128, 128), bf16),
-        pltpu.VMEM((2, 2, 128, 128), bf16),
-        pltpu.VMEM((2, 2, 2, 128, 128), bf16),
+        pltpu.VMEM((2, 4, 2, 128, 128), bf16),
         pltpu.VMEM((4, 3, 2, 32, 128), bf16),
         pltpu.VMEM((4, 2, 32, 128), f32),
         pltpu.VMEM((16, 32, 128), f32),

time: 71.8 us -> 77.4 us (1.078)
  the two profiles are of different devices: /device:TPU:4 before, /device:TPU:1 now
where the time goes in v3:
time: 77.4 us; the launch traced here: 77.2 us
  Pallas kernels  72.2 us (93%)
  local copies, waits for them, and re-layouts  3.74 us (5%)
  between operations  1.29 us (2%)
    pallas_call x1, Pallas kernels, body(): call(pair, length, ln_gain.reshape(1, 128), w_query, w_key, w_value, w_ga...  72.2 us
    unnamed x2, local copies, waits for them, and re-layouts  3.74 us

profile of v3, /device:TPU:1, one launch (start us, length us, event | category | flops | bytes accessed | tf_op | source)
XLA Modules:
  0.0 77.2 jit_solution(8571701343809295182)
XLA Ops:
  1.3 72.2 %shard_map.113 = (bf16[8,32,128]{2,1,0:T(8,128)(2,1)}, f32[64,32,128]{2,1,0:T(8,128)}) custom-call(bf16[64,32,128]{2,1,0:T(8,128)(2,1)} %pair_h.1, s32[1]{0:T(128)S(6)} %copy.14.length, f32[1,128]{1,0:T(1,128)} %bitcast.3, bf16[128,128]{1,0:T(8,128)(2,1)} %w_query_h.1, bf16[128,128]{1,0:T(8,128)(2,1)} %w_key_h.1, bf16[128,128]{1,0:T(8,128)(2,1)} %w_value_h.1, ...), custom_call_target="tpu_custom_call" | custom-call | tf_op jit(solution)/shard_map/pallas_call | solution.py:465
  73.5 1.5 %copy.15 = bf16[8,32,128]{2,1,0:T(8,128)(2,1)} copy(bf16[8,32,128]{2,1,0:T(8,128)(2,1)} %get-tuple-element.4) | data formatting | bytes 131072
  74.9 2.3 %copy.16 = f32[64,32,128]{2,1,0:T(8,128)} copy(f32[64,32,128]{2,1,0:T(8,128)} %get-tuple-element.5) | data formatting | bytes 2097152

commit v4 on v3

--- a/solution.py
+++ b/solution.py
@@ -12,7 +12,7 @@
 bf16 = jnp.bfloat16
 COPIES = (
     ("kvz", 4), ("qdz", 4), ("bt", 16), ("kvx", 4), ("kvc", 4), ("ya", 8), ("dkvc", 2), ("dr", 8),
-    ("yr", 8), ("dt", 16), ("oz", 4), ("dqz", 4), ("dkvz", 4),
+    ("yr", 8), ("dt", 2), ("dbz", 8), ("oz", 4), ("dqz", 4), ("dkvz", 4),
 )
 
 AROUND = ((0, 0), (0, 1), (0, 3), (0, 2), (1, 0), (1, 1), (1, 3), (1, 2))
@@ -54,7 +54,7 @@
     pair_h, length, gain, w_query_h, w_key_h, w_value_h, w_gate_h, w_bias, w_out_h, out_grad_h,
     update, pair_grad,
     pair, w_query, w_key, w_value, w_gate, w_out, out_grad, load_sem, xhat, rstd_all, w_rows, gate_s, gg_s, zsend, kv, qd, qdt, bsend, brecv, bias, bias_f,
-    dbias, att, dqkv, db_send, db_y, db_out, db_in, dkv_send, dkv_c, dkv_m, dkv_in,
+    dbias, att, dqkv, db_send, db_y, db_s, db_t, db_out, db_in, dkv_send, dkv_c, dkv_m, dkv_in,
     e_in, o_in, gw,
     *sems,
 ):
@@ -87,12 +87,18 @@
     def y_dev(d):
         return device(y_at(d) * 2 + zhi, x, z, core)
 
+    def zz_dev(e, d):
+        return device(y * 2 + lax.rem(zhi + e, 2), x, z_at(d), core)
+
     def by_column(e, d, c):
         return device(blk * 2 + lax.rem(zhi + e, 2), lax.div(y, 2), z_at(d), c)
 
-    def by_row(e, d, s):
+    def by_row_all(e, d, s):
         return device(
             (x * 2 + s) * 2 + lax.rem(zhi + e, 2), lax.div(y, 2), z_at(d), lax.rem(y, 2))
+
+    def by_row(s):
+        return device((x * 2 + s) * 2 + zhi, lax.div(y, 2), z, lax.rem(y, 2))
 
     core_dev = device(row, x, z, other)
     stays = blk == y
@@ -134,9 +140,9 @@
     barrier = pltpu.get_barrier_semaphore()
     turns = [(e, d, other) for e in range(2) for d in range(4)]
     turns += [(e, d, core) for e in range(2) for d in range(4) if (e, d) != (0, 0)]
-    partners = [z_dev(d) for d in (1, 2, 3)] + [core_dev] + [x_dev(d) for d in (1, 2, 3)]
-    partners += [y_dev(d) for d in range(1, 8)]
-    partners += [by_column(*turn) for turn in turns] + [by_row(*turn) for turn in turns]
+    partners = [zz_dev(e, d) for e, d in AROUND[1:]]
+    partners += [core_dev] + [x_dev(d) for d in (1, 2, 3)] + [y_dev(d) for d in range(1, 8)]
+    partners += [by_row_all(*turn) for turn in turns] + [by_column(0, 0, other)]
 
     def greet(dev):
         pl.semaphore_signal(barrier, inc=1, device_id=dev, device_id_type=MESH)
@@ -147,7 +153,7 @@
     @pl.when(jnp.logical_not(stays))
     def _():
         greet(by_column(0, 0, core))
-        greet(by_row(0, 0, core))
+        greet(by_row(core))
 
     gain_v = gain[...]
     for copy in loads:
@@ -268,7 +274,7 @@
             send(dkv_m.at[g, x_at(d)], dkv_in.at[g, d], "dr", g * 4 + d, x_dev(d))
 
     for g in range(2):
-        def attend(a, carry):
+        def attend(a):
             own = lanes == a
             key = kv[:, 0, g].reshape(1024, 128)
             value = kv[:, 1, g].reshape(1024, 128)
@@ -290,18 +296,17 @@
             grads_b = grads.astype(bf16)
             dq = nn(grads_b, key) * (32 ** (-0.5))
             dqkv[0, g] = jnp.where(own, dq, dqkv[0, g].astype(f32)).astype(bf16)
-            part = pl.ds(pl.multiple_of(a * 32, 32), 32)
+            part = slice(a * 32, (a + 1) * 32)
             dk = nn(qdt[0, g, part, :], grads_b).astype(bf16)
             dv = nn(qdt[1, g, part, :], shares.astype(bf16)).astype(bf16)
             for b in range(8):
                 dkv_send[b % 2, g, b // 2, 0, part, :] = dk[:, b * 128:(b + 1) * 128]
                 dkv_send[b % 2, g, b // 2, 1, part, :] = dv[:, b * 128:(b + 1) * 128]
-            return carry
-
-        lax.fori_loop(0, 2, attend, 0)
-        if g == 1:
-            cores_summed(0)
-        lax.fori_loop(2, 4, attend, 0)
+
+        for a in range(4):
+            if (g, a) == (1, 2):
+                cores_summed(0)
+            attend(a)
         send(dkv_send.at[other, g], dkv_c.at[g], "dkvc", g, core_dev)
 
     for b in range(8):
@@ -321,19 +326,9 @@
     for d in range(1, 8):
         arrived(db_y.at[d], "yr", d)
         total = total + db_y[d].astype(f32)
-    total = total.reshape(2, 2, 2, 16, 128)
-    for n in range(2):
-        for e in range(2):
-            tiles = [jnp.where(core == c, total[n, e, i], 0.0) for c in range(2) for i in range(2)]
-            outs = lane_swap(tiles)
-            for b in range(4):
-                db_out[n, e, b] = outs[b]
-    turn_own(db_out.at[core, zhi, z], db_in.at[core, zhi, z], "dt", core * 8, by_row(0, 0, core))
-    for n, c in enumerate((core, other)):
-        for e, d in AROUND:
-            if (n, e, d) != (0, 0, 0):
-                send(db_out.at[c, lax.rem(zhi + e, 2), z_at(d)], db_in.at[core, zhi, z], "dt",
-                     n * 8 + e * 4 + d, by_row(e, d, c), core * 8 + e * 4 + d)
+    db_s[...] = total.reshape(2, 64, 128)
+    turn_own(db_s.at[core], db_t.at[core], "dt", core, by_row(core))
+    send(db_s.at[other], db_t.at[core], "dt", 1, by_row(other), core)
 
     for g in range(2):
         for d in (1, 3, 2):
@@ -347,6 +342,18 @@
         rows_d = pl.ds(pl.multiple_of(z_at(d) * 32, 32), 32)
         send(dqkv.at[1:3, :, rows_d, :], e_in.at[z, 1:3], "dkvz", d, z_dev(d))
     e_in[z, 1:3] = dqkv[1:3, :, z_rows, :]
+
+    arrived(db_t.at[0], "dt", 0)
+    arrived(db_t.at[1], "dt", 1)
+    for e in range(2):
+        final = db_t[:, e * 32:(e + 1) * 32, :].reshape(64, 128)
+        outs = lane_swap([final[q * 16:(q + 1) * 16] for q in range(4)])
+        for b in range(4):
+            db_out[e, b] = outs[b]
+    for e, d in AROUND[1:]:
+        send(db_out.at[lax.rem(zhi + e, 2), z_at(d)], db_in.at[zhi, z], "dbz", e * 4 + d,
+             zz_dev(e, d))
+    db_in[zhi, z] = db_out[zhi, z]
 
     for d in (1, 2, 3):
         h_d = z_at(4 - d)
@@ -375,10 +382,9 @@
     gw[0:8] = grad_window.reshape(8, 32, 128)
     gw[8:16] = jnp.zeros((8, 32, 128), f32)
 
-    for n in range(2):
-        for e, d in AROUND:
-            arrived(db_in.at[n, lax.rem(zhi + e, 2), z_at(4 - d)], "dt", n * 8 + e * 4 + d)
-    flat = ((db_in[0, 0] + db_in[0, 1]) + (db_in[1, 0] + db_in[1, 1])).reshape(64, 128).T
+    for e, d in AROUND[1:]:
+        arrived(db_in.at[lax.rem(zhi + e, 2), z_at(4 - d)], "dbz", e * 4 + d)
+    flat = (db_in[0] + db_in[1]).reshape(64, 128).T
     high = flat.astype(bf16)
     rest = flat - high.astype(f32)
     mid = rest.astype(bf16)
@@ -437,8 +443,10 @@
         pltpu.VMEM((3, 2, 128, 128), bf16),
         pltpu.VMEM((8, 128, 128), bf16),
         pltpu.VMEM((8, 128, 128), bf16),
-        pltpu.VMEM((2, 2, 4, 16, 128), f32),
-        pltpu.VMEM((2, 2, 4, 16, 128), f32),
+        pltpu.VMEM((2, 64, 128), f32),
+        pltpu.VMEM((2, 64, 128), f32),
+        pltpu.VMEM((2, 4, 16, 128), f32),
+        pltpu.VMEM((2, 4, 16, 128), f32),
         pltpu.VMEM((2, 2, 4, 2, 128, 128), bf16),
         pltpu.VMEM((2, 4, 2, 128, 128), bf16),
         pltpu.VMEM((2, 4, 2, 128, 128), bf16),

time: 77.4 us -> 70.7 us (0.913)
  the two profiles are of different devices: /device:TPU:1 before, /device:TPU:4 now
where the time goes in v4:
time: 70.7 us; the launch traced here: 70.5 us
  Pallas kernels  65.4 us (93%)
  local copies, waits for them, and re-layouts  3.74 us (5%)
  between operations  1.29 us (2%)
    pallas_call x1, Pallas kernels, body(): call(pair, length, ln_gain.reshape(1, 128), w_query, w_key, w_value, w_ga...  65.4 us
    unnamed x2, local copies, waits for them, and re-layouts  3.74 us

profile of v4, /device:TPU:4, one launch (start us, length us, event | category | flops | bytes accessed | tf_op | source)
XLA Modules:
  0.0 70.5 jit_solution(1418187150625736280)
XLA Ops:
  1.3 65.4 %shard_map.113 = (bf16[8,32,128]{2,1,0:T(8,128)(2,1)}, f32[64,32,128]{2,1,0:T(8,128)}) custom-call(bf16[64,32,128]{2,1,0:T(8,128)(2,1)} %pair_h.1, s32[1]{0:T(128)S(6)} %copy.14.length, f32[1,128]{1,0:T(1,128)} %bitcast.3, bf16[128,128]{1,0:T(8,128)(2,1)} %w_query_h.1, bf16[128,128]{1,0:T(8,128)(2,1)} %w_key_h.1, bf16[128,128]{1,0:T(8,128)(2,1)} %w_value_h.1, ...), custom_call_target="tpu_custom_call" | custom-call | tf_op jit(solution)/shard_map/pallas_call | solution.py:473
  66.7 1.5 %copy.15 = bf16[8,32,128]{2,1,0:T(8,128)(2,1)} copy(bf16[8,32,128]{2,1,0:T(8,128)(2,1)} %get-tuple-element.4) | data formatting | bytes 131072
  68.2 2.3 %copy.16 = f32[64,32,128]{2,1,0:T(8,128)} copy(f32[64,32,128]{2,1,0:T(8,128)} %get-tuple-element.5) | data formatting | bytes 2097152

commit v5 on v4

--- a/solution.py
+++ b/solution.py
@@ -128,6 +128,24 @@
     def arrived(slot, name, n):
         remote(slot, slot, sem[name][0].at[n], sem[name][1].at[n], core_dev).wait_recv()
 
+    barrier = pltpu.get_barrier_semaphore()
+    turns = [(e, d, other) for e in range(2) for d in range(4)]
+    turns += [(e, d, core) for e in range(2) for d in range(4) if (e, d) != (0, 0)]
+    partners = [by_row_all(*turn) for turn in reversed(turns)] + [by_column(0, 0, other)]
+    partners += [y_dev(d) for d in (4, 3, 5, 2, 6, 1, 7)] + [x_dev(d) for d in (2, 1, 3)]
+    partners += [zz_dev(e, d) for e, d in reversed(AROUND[1:])] + [core_dev]
+
+    def greet(dev):
+        pl.semaphore_signal(barrier, inc=1, device_id=dev, device_id_type=MESH)
+
+    @pl.when(jnp.logical_not(stays))
+    def _():
+        greet(by_column(0, 0, core))
+        greet(by_row(core))
+
+    for dev in partners:
+        greet(dev)
+
     loads = [
         pltpu.make_async_copy(src, dst, load_sem.at[n])
         for n, (src, dst) in enumerate((
@@ -136,24 +154,6 @@
     ]
     for copy in loads:
         copy.start()
-
-    barrier = pltpu.get_barrier_semaphore()
-    turns = [(e, d, other) for e in range(2) for d in range(4)]
-    turns += [(e, d, core) for e in range(2) for d in range(4) if (e, d) != (0, 0)]
-    partners = [zz_dev(e, d) for e, d in AROUND[1:]]
-    partners += [core_dev] + [x_dev(d) for d in (1, 2, 3)] + [y_dev(d) for d in range(1, 8)]
-    partners += [by_row_all(*turn) for turn in turns] + [by_column(0, 0, other)]
-
-    def greet(dev):
-        pl.semaphore_signal(barrier, inc=1, device_id=dev, device_id_type=MESH)
-
-    for dev in partners:
-        greet(dev)
-
-    @pl.when(jnp.logical_not(stays))
-    def _():
-        greet(by_column(0, 0, core))
-        greet(by_row(core))
 
     gain_v = gain[...]
     for copy in loads:
@@ -183,14 +183,6 @@
             for h in range(4):
                 zsend[h, n, g] = outs[h].astype(bf16)
 
-    pl.semaphore_wait(barrier, len(partners) + jnp.where(stays, 0, 2))
-
-    z_rows = pl.ds(pl.multiple_of(z * 32, 32), 32)
-    for d in (1, 3, 2):
-        send(zsend.at[z_at(d), 0:2], kv.at[blk, :, :, z_rows, :], "kvz", d, z_dev(d))
-    kv[blk, :, :, z_rows, :] = zsend[z, 0:2]
-    qd[:, :, z_rows, :] = zsend[z, 2:4]
-
     pick = lax.broadcasted_iota(jnp.int32, (64, 4), 0) // 16 == lax.broadcasted_iota(
         jnp.int32, (64, 4), 1)
     w_rows[...] = nn(pick.astype(bf16), w_bias[...]).astype(bf16)
@@ -210,6 +202,14 @@
 
     tile_bias = lax.fori_loop(0, 4, tile_step, jnp.zeros((64, 128), f32))
     bsend[...] = tile_bias.astype(bf16).reshape(4, 16, 128)
+    pl.semaphore_wait(barrier, len(partners) + jnp.where(stays, 0, 2))
+
+    z_rows = pl.ds(pl.multiple_of(z * 32, 32), 32)
+    for d in (1, 3, 2):
+        send(zsend.at[z_at(d), 0:2], kv.at[blk, :, :, z_rows, :], "kvz", d, z_dev(d))
+    kv[blk, :, :, z_rows, :] = zsend[z, 0:2]
+    qd[:, :, z_rows, :] = zsend[z, 2:4]
+
     odd = lax.rem(y, 2)
     turn_own(bsend.at[z], brecv.at[odd, zhi, z], "bt", odd * 8, by_column(0, 0, core))
     for n, c in enumerate((core, other)):

time: 70.7 us -> 70.3 us (level)
  the two profiles are of different devices: /device:TPU:4 before, /device:TPU:14 now
where the time goes in v5:
time: 70.3 us; the launch traced here: 70 us
  Pallas kernels  65 us (92%)
  local copies, waits for them, and re-layouts  3.74 us (5%)
  between operations  1.29 us (2%)
    pallas_call x1, Pallas kernels, body(): call(pair, length, ln_gain.reshape(1, 128), w_query, w_key, w_value, w_ga...  65 us
    unnamed x2, local copies, waits for them, and re-layouts  3.74 us

profile of v5, /device:TPU:14, one launch (start us, length us, event | category | flops | bytes accessed | tf_op | source)
XLA Modules:
  0.0 70.0 jit_solution(17159648591736401147)
XLA Ops:
  1.3 65.0 %shard_map.113 = (bf16[8,32,128]{2,1,0:T(8,128)(2,1)}, f32[64,32,128]{2,1,0:T(8,128)}) custom-call(bf16[64,32,128]{2,1,0:T(8,128)(2,1)} %pair_h.1, s32[1]{0:T(128)S(6)} %copy.14.length, f32[1,128]{1,0:T(1,128)} %bitcast.3, bf16[128,128]{1,0:T(8,128)(2,1)} %w_query_h.1, bf16[128,128]{1,0:T(8,128)(2,1)} %w_key_h.1, bf16[128,128]{1,0:T(8,128)(2,1)} %w_value_h.1, ...), custom_call_target="tpu_custom_call" | custom-call | tf_op jit(solution)/shard_map/pallas_call | solution.py:473
  66.3 1.5 %copy.15 = bf16[8,32,128]{2,1,0:T(8,128)(2,1)} copy(bf16[8,32,128]{2,1,0:T(8,128)(2,1)} %get-tuple-element.4) | data formatting | bytes 131072
  67.7 2.3 %copy.16 = f32[64,32,128]{2,1,0:T(8,128)} copy(f32[64,32,128]{2,1,0:T(8,128)} %get-tuple-element.5) | data formatting | bytes 2097152

commit v6 on v5

--- a/solution.py
+++ b/solution.py
@@ -55,7 +55,7 @@
     update, pair_grad,
     pair, w_query, w_key, w_value, w_gate, w_out, out_grad, load_sem, xhat, rstd_all, w_rows, gate_s, gg_s, zsend, kv, qd, qdt, bsend, brecv, bias, bias_f,
     dbias, att, dqkv, db_send, db_y, db_s, db_t, db_out, db_in, dkv_send, dkv_c, dkv_m, dkv_in,
-    e_in, o_in, gw,
+    e_in, o_in, gw, raw_s, raw_p, grads_s, shares_s, result_s, leave_sem,
     *sems,
 ):
     sem = {name: sems[2 * n:2 * n + 2] for n, (name, _) in enumerate(COPIES)}
@@ -252,6 +252,14 @@
     for d in (0, 1, 3, 2):
         arrived(kv.at[x_at(4 - d) * 2 + other], "kvc", d)
 
+    lanes = lane_block((128, 128))
+    for g in range(2):
+        for a in range(4):
+            q_a = jnp.where(lanes == a, qd[0, g].astype(f32), 0.0).astype(bf16)
+            do_a = jnp.where(lanes == a, qd[1, g].astype(f32), 0.0).astype(bf16)
+            raw_s[g * 4 + a] = nt(q_a, kv[:, 0, g].reshape(1024, 128))
+            raw_p[g * 4 + a] = nt(do_a, kv[:, 1, g].reshape(1024, 128))
+
     for d in range(1, 8):
         arrived(bias.at[y_at(8 - d)], "ya", d)
 
@@ -264,7 +272,6 @@
     dbias[...] = jnp.zeros_like(dbias)
     att[...] = jnp.zeros_like(att)
     dqkv[0] = jnp.zeros_like(dqkv[0])
-    lanes = lane_block((128, 128))
 
     def cores_summed(g):
         arrived(dkv_c.at[g], "dkvc", g)
@@ -274,40 +281,23 @@
             send(dkv_m.at[g, x_at(d)], dkv_in.at[g, d], "dr", g * 4 + d, x_dev(d))
 
     for g in range(2):
-        def attend(a):
+        for a in range(4):
             own = lanes == a
-            key = kv[:, 0, g].reshape(1024, 128)
-            value = kv[:, 1, g].reshape(1024, 128)
-            q_a = jnp.where(own, qd[0, g].astype(f32), 0.0).astype(bf16)
             do_f = jnp.where(own, qd[1, g].astype(f32), 0.0)
-            do_a = do_f.astype(bf16)
-            logits = jnp.where(keep, nt(q_a, key) + bias_f[...], NEG)
+            logits = jnp.where(keep, raw_s[g * 4 + a] + bias_f[...], NEG)
             top = jnp.max(logits, axis=-1, keepdims=True)
             expo = jnp.exp(logits - top)
             inv = 1.0 / jnp.sum(expo, axis=-1, keepdims=True)
-            out = nn(expo.astype(bf16), value) * inv
+            out = nn(expo.astype(bf16), kv[:, 1, g].reshape(1024, 128)) * inv
             out = jnp.where(own, out, 0.0)
             att[g] = att[g] + out
             delta = jnp.sum(do_f * out, axis=-1, keepdims=True)
             shares = expo * inv
-            grads = shares * (nt(do_a, value) - delta)
+            grads = shares * (raw_p[g * 4 + a] - delta)
             for b in range(8):
                 dbias[b] = dbias[b] + grads[:, b * 128:(b + 1) * 128]
-            grads_b = grads.astype(bf16)
-            dq = nn(grads_b, key) * (32 ** (-0.5))
-            dqkv[0, g] = jnp.where(own, dq, dqkv[0, g].astype(f32)).astype(bf16)
-            part = slice(a * 32, (a + 1) * 32)
-            dk = nn(qdt[0, g, part, :], grads_b).astype(bf16)
-            dv = nn(qdt[1, g, part, :], shares.astype(bf16)).astype(bf16)
-            for b in range(8):
-                dkv_send[b % 2, g, b // 2, 0, part, :] = dk[:, b * 128:(b + 1) * 128]
-                dkv_send[b % 2, g, b // 2, 1, part, :] = dv[:, b * 128:(b + 1) * 128]
-
-        for a in range(4):
-            if (g, a) == (1, 2):
-                cores_summed(0)
-            attend(a)
-        send(dkv_send.at[other, g], dkv_c.at[g], "dkvc", g, core_dev)
+            grads_s[g * 4 + a] = grads.astype(bf16)
+            shares_s[g * 4 + a] = shares.astype(bf16)
 
     for b in range(8):
         db_send[b] = dbias[b].astype(bf16)
@@ -316,17 +306,33 @@
     for d in (1, 3, 2):
         rows_d = pl.ds(pl.multiple_of(z_at(d) * 32, 32), 32)
         send(att.at[:, rows_d, :], o_in.at[z], "oz", d, z_dev(d))
+    o_in[z] = att[:, z_rows, :]
+
+    for g in range(2):
+        for a in range(4):
+            if (g, a) == (1, 2):
+                cores_summed(0)
+            grads = grads_s[g * 4 + a]
+            dq = nn(grads, kv[:, 0, g].reshape(1024, 128)) * (32 ** (-0.5))
+            dqkv[0, g] = jnp.where(lanes == a, dq, dqkv[0, g].astype(f32)).astype(bf16)
+            part = slice(a * 32, (a + 1) * 32)
+            dk = nn(qdt[0, g, part, :], grads).astype(bf16)
+            dv = nn(qdt[1, g, part, :], shares_s[g * 4 + a]).astype(bf16)
+            for b in range(8):
+                dkv_send[b % 2, g, b // 2, 0, part, :] = dk[:, b * 128:(b + 1) * 128]
+                dkv_send[b % 2, g, b // 2, 1, part, :] = dv[:, b * 128:(b + 1) * 128]
+        send(dkv_send.at[other, g], dkv_c.at[g], "dkvc", g, core_dev)
+    for d in (1, 3, 2):
+        rows_d = pl.ds(pl.multiple_of(z_at(d) * 32, 32), 32)
         send(dqkv.at[0, :, rows_d, :], e_in.at[z, 0], "dqz", d, z_dev(d))
-    o_in[z] = att[:, z_rows, :]
     e_in[z, 0] = dqkv[0, :, z_rows, :]
-
     cores_summed(1)
 
     total = dbias[y]
     for d in range(1, 8):
         arrived(db_y.at[d], "yr", d)
         total = total + db_y[d].astype(f32)
-    db_s[...] = total.reshape(2, 64, 128)
+    db_s[...] = total.reshape(2, 64, 128).astype(bf16)
     turn_own(db_s.at[core], db_t.at[core], "dt", core, by_row(core))
     send(db_s.at[other], db_t.at[core], "dt", 1, by_row(other), core)
 
@@ -346,7 +352,7 @@
     arrived(db_t.at[0], "dt", 0)
     arrived(db_t.at[1], "dt", 1)
     for e in range(2):
-        final = db_t[:, e * 32:(e + 1) * 32, :].reshape(64, 128)
+        final = db_t[:, e * 32:(e + 1) * 32, :].astype(f32).reshape(64, 128)
         outs = lane_swap([final[q * 16:(q + 1) * 16] for q in range(4)])
         for b in range(4):
             db_out[e, b] = outs[b]
@@ -390,6 +396,10 @@
     mid = rest.astype(bf16)
     low = (rest - mid.astype(f32)).astype(bf16)
 
+    def leave(i):
+        part = pl.ds(i * 2, 2)
+        return pltpu.make_async_copy(result_s.at[:, part], pair_grad.at[:, part], leave_sem.at[i])
+
     def final_step(i, carry):
         for u in range(2):
             jj = i * 2 + u
@@ -401,10 +411,13 @@
             second = jnp.mean(grad * hat, axis=-1, keepdims=True)
             result = rstd_all[jj] * (grad - first - hat * second)
             for q in range(4):
-                pair_grad[q * 16 + jj] = result[q * 32:(q + 1) * 32]
+                result_s[q, jj] = result[q * 32:(q + 1) * 32]
+        leave(i).start()
         return carry
 
     lax.fori_loop(0, 8, final_step, 0)
+    for i in range(8):
+        leave(i).wait()
 
     for copy in sent:
         copy.wait_send()
@@ -443,8 +456,8 @@
         pltpu.VMEM((3, 2, 128, 128), bf16),
         pltpu.VMEM((8, 128, 128), bf16),
         pltpu.VMEM((8, 128, 128), bf16),
-        pltpu.VMEM((2, 64, 128), f32),
-        pltpu.VMEM((2, 64, 128), f32),
+        pltpu.VMEM((2, 64, 128), bf16),
+        pltpu.VMEM((2, 64, 128), bf16),
         pltpu.VMEM((2, 4, 16, 128), f32),
         pltpu.VMEM((2, 4, 16, 128), f32),
         pltpu.VMEM((2, 2, 4, 2, 128, 128), bf16),
@@ -454,6 +467,12 @@
         pltpu.VMEM((4, 3, 2, 32, 128), bf16),
         pltpu.VMEM((4, 2, 32, 128), f32),
         pltpu.VMEM((16, 32, 128), f32),
+        pltpu.VMEM((8, 128, 1024), f32),
+        pltpu.VMEM((8, 128, 1024), f32),
+        pltpu.VMEM((8, 128, 1024), bf16),
+        pltpu.VMEM((8, 128, 1024), bf16),
+        pltpu.VMEM((4, 16, 32, 128), f32),
+        pltpu.SemaphoreType.DMA((8,)),
     ]
     for _, n in COPIES:
         scratch += [pltpu.SemaphoreType.DMA((n,)), pltpu.SemaphoreType.DMA((n,))]
@@ -461,19 +480,20 @@
         kernel,
         out_shape=(
             jax.ShapeDtypeStruct(out_grad.shape, bf16),
-            jax.ShapeDtypeStruct(pair.shape, f32),
+            jax.ShapeDtypeStruct((4, 16, 32, 128), f32),
         ),
         in_specs=[hbm, smem, vmem, hbm, hbm, hbm, hbm, vmem, hbm, hbm],
-        out_specs=(vmem, vmem),
+        out_specs=(vmem, hbm),
         scratch_shapes=scratch,
         compiler_params=pltpu.CompilerParams(
             collective_id=0, has_side_effects=True, vmem_limit_bytes=63 * 1024 * 1024
         ),
     )
-    return call(
+    update, pair_grad = call(
         pair, length, ln_gain.reshape(1, 128), w_query, w_key, w_value, w_gate, w_bias.T, w_out,
         out_grad,
     )
+    return update, pair_grad.reshape(pair.shape)
 
 
 def solution(mesh):

time: 70.3 us -> 65.6 us (0.933)
  the two profiles are of different devices: /device:TPU:14 before, /device:TPU:1 now
where the time goes in v6:
time: 65.6 us; the launch traced here: 64.4 us
  Pallas kernels  59.4 us (91%)
  local copies, waits for them, and re-layouts  3.74 us (6%)
  between operations  1.29 us (2%)
    pallas_call x1, Pallas kernels, body(): call(pair, length, ln_gain.reshape(1, 128), w_query, w_key, w_value, w_ga...  59.4 us
    unnamed x2, local copies, waits for them, and re-layouts  3.74 us

profile of v6, /device:TPU:1, one launch (start us, length us, event | category | flops | bytes accessed | tf_op | source)
XLA Modules:
  0.0 64.4 jit_solution(12325640914240593793)
XLA Ops:
  1.3 59.4 %shard_map.113 = (bf16[8,32,128]{2,1,0:T(8,128)(2,1)}, f32[4,16,32,128]{3,2,1,0:T(8,128)}) custom-call(bf16[64,32,128]{2,1,0:T(8,128)(2,1)} %pair_h.1, s32[1]{0:T(128)S(6)} %copy.14.length, f32[1,128]{1,0:T(1,128)} %bitcast.5, bf16[128,128]{1,0:T(8,128)(2,1)} %w_query_h.1, bf16[128,128]{1,0:T(8,128)(2,1)} %w_key_h.1, bf16[128,128]{1,0:T(8,128)(2,1)} %w_value_h.1, ...), custom_call_target="tpu_custom_call" | custom-call | tf_op jit(solution)/shard_map/pallas_call | solution.py:492
  60.7 1.5 %copy.15 = bf16[8,32,128]{2,1,0:T(8,128)(2,1)} copy(bf16[8,32,128]{2,1,0:T(8,128)(2,1)} %get-tuple-element.8) | data formatting | bytes 131072
  62.2 2.3 %copy.16 = f32[64,32,128]{2,1,0:T(8,128)} copy(f32[64,32,128]{2,1,0:T(8,128)} %bitcast.3) | data formatting | bytes 2097152

commit v7 on v6

--- a/solution.py
+++ b/solution.py
@@ -56,6 +56,7 @@
     pair, w_query, w_key, w_value, w_gate, w_out, out_grad, load_sem, xhat, rstd_all, w_rows, gate_s, gg_s, zsend, kv, qd, qdt, bsend, brecv, bias, bias_f,
     dbias, att, dqkv, db_send, db_y, db_s, db_t, db_out, db_in, dkv_send, dkv_c, dkv_m, dkv_in,
     e_in, o_in, gw, raw_s, raw_p, grads_s, shares_s, result_s, leave_sem,
+    update_s,
     *sems,
 ):
     sem = {name: sems[2 * n:2 * n + 2] for n, (name, _) in enumerate(COPIES)}
@@ -204,12 +205,6 @@
     bsend[...] = tile_bias.astype(bf16).reshape(4, 16, 128)
     pl.semaphore_wait(barrier, len(partners) + jnp.where(stays, 0, 2))
 
-    z_rows = pl.ds(pl.multiple_of(z * 32, 32), 32)
-    for d in (1, 3, 2):
-        send(zsend.at[z_at(d), 0:2], kv.at[blk, :, :, z_rows, :], "kvz", d, z_dev(d))
-    kv[blk, :, :, z_rows, :] = zsend[z, 0:2]
-    qd[:, :, z_rows, :] = zsend[z, 2:4]
-
     odd = lax.rem(y, 2)
     turn_own(bsend.at[z], brecv.at[odd, zhi, z], "bt", odd * 8, by_column(0, 0, core))
     for n, c in enumerate((core, other)):
@@ -217,6 +212,12 @@
             if (n, e, d) != (0, 0, 0):
                 send(bsend.at[z_at(d)], brecv.at[odd, zhi, z], "bt", n * 8 + e * 4 + d,
                      by_column(e, d, c), odd * 8 + e * 4 + d)
+    z_rows = pl.ds(pl.multiple_of(z * 32, 32), 32)
+    for d in (1, 3, 2):
+        send(zsend.at[z_at(d), 0:2], kv.at[blk, :, :, z_rows, :], "kvz", d, z_dev(d))
+    kv[blk, :, :, z_rows, :] = zsend[z, 0:2]
+    qd[:, :, z_rows, :] = zsend[z, 2:4]
+
     for d in (1, 3, 2):
         send(zsend.at[z_at(d), 2:4], qd.at[:, :, z_rows, :], "qdz", d, z_dev(d))
 
@@ -313,8 +314,6 @@
             if (g, a) == (1, 2):
                 cores_summed(0)
             grads = grads_s[g * 4 + a]
-            dq = nn(grads, kv[:, 0, g].reshape(1024, 128)) * (32 ** (-0.5))
-            dqkv[0, g] = jnp.where(lanes == a, dq, dqkv[0, g].astype(f32)).astype(bf16)
             part = slice(a * 32, (a + 1) * 32)
             dk = nn(qdt[0, g, part, :], grads).astype(bf16)
             dv = nn(qdt[1, g, part, :], shares_s[g * 4 + a]).astype(bf16)
@@ -322,6 +321,10 @@
                 dkv_send[b % 2, g, b // 2, 0, part, :] = dk[:, b * 128:(b + 1) * 128]
                 dkv_send[b % 2, g, b // 2, 1, part, :] = dv[:, b * 128:(b + 1) * 128]
         send(dkv_send.at[other, g], dkv_c.at[g], "dkvc", g, core_dev)
+    for g in range(2):
+        for a in range(4):
+            dq = nn(grads_s[g * 4 + a], kv[:, 0, g].reshape(1024, 128)) * (32 ** (-0.5))
+            dqkv[0, g] = jnp.where(lanes == a, dq, dqkv[0, g].astype(f32)).astype(bf16)
     for d in (1, 3, 2):
         rows_d = pl.ds(pl.multiple_of(z_at(d) * 32, 32), 32)
         send(dqkv.at[0, :, rows_d, :], e_in.at[z, 0], "dqz", d, z_dev(d))
@@ -374,7 +377,9 @@
             gate_t, gg_t = gate_s[at], gg_s[at]
             gated.append((gate_t * outs[i]).astype(bf16))
             pres.append((gg_t * outs[i] * gate_t * (1.0 - gate_t)).astype(bf16))
-    update[...] = nn(jnp.concatenate(gated, axis=0), w_out[...]).astype(bf16).reshape(8, 32, 128)
+    update_s[...] = nn(jnp.concatenate(gated, axis=0), w_out[...]).astype(bf16).reshape(8, 32, 128)
+    update_out = pltpu.make_async_copy(update_s, update, leave_sem.at[4])
+    update_out.start()
     for d in (1, 2, 3):
         arrived(e_in.at[z_at(4 - d), 1:3], "dkvz", d)
     sides = [jnp.concatenate(pres, axis=0)]
@@ -388,6 +393,8 @@
     gw[0:8] = grad_window.reshape(8, 32, 128)
     gw[8:16] = jnp.zeros((8, 32, 128), f32)
 
+    for copy in sent[:-7]:
+        copy.wait_send()
     for e, d in AROUND[1:]:
         arrived(db_in.at[lax.rem(zhi + e, 2), z_at(4 - d)], "dbz", e * 4 + d)
     flat = (db_in[0] + db_in[1]).reshape(64, 128).T
@@ -397,12 +404,12 @@
     low = (rest - mid.astype(f32)).astype(bf16)
 
     def leave(i):
-        part = pl.ds(i * 2, 2)
+        part = pl.ds(i * 4, 4)
         return pltpu.make_async_copy(result_s.at[:, part], pair_grad.at[:, part], leave_sem.at[i])
 
     def final_step(i, carry):
-        for u in range(2):
-            jj = i * 2 + u
+        for u in range(4):
+            jj = i * 4 + u
             chosen = jnp.where(row_in == jj, w_rows[...].astype(f32), 0.0).astype(bf16)
             grad = nn(high, chosen) + (nn(mid, chosen) + nn(low, chosen))
             grad = jnp.concatenate([grad[0:32] + gw[jj], grad[32:]], axis=0) * gain_v
@@ -415,11 +422,12 @@
         leave(i).start()
         return carry
 
-    lax.fori_loop(0, 8, final_step, 0)
-    for i in range(8):
+    lax.fori_loop(0, 4, final_step, 0)
+    for i in range(4):
         leave(i).wait()
-
-    for copy in sent:
+    update_out.wait()
+
+    for copy in sent[-7:]:
         copy.wait_send()
 
     @pl.when(jnp.logical_not(stays))
@@ -472,7 +480,8 @@
         pltpu.VMEM((8, 128, 1024), bf16),
         pltpu.VMEM((8, 128, 1024), bf16),
         pltpu.VMEM((4, 16, 32, 128), f32),
-        pltpu.SemaphoreType.DMA((8,)),
+        pltpu.SemaphoreType.DMA((5,)),
+        pltpu.VMEM(out_grad.shape, bf16),
     ]
     for _, n in COPIES:
         scratch += [pltpu.SemaphoreType.DMA((n,)), pltpu.SemaphoreType.DMA((n,))]
@@ -483,7 +492,7 @@
             jax.ShapeDtypeStruct((4, 16, 32, 128), f32),
         ),
         in_specs=[hbm, smem, vmem, hbm, hbm, hbm, hbm, vmem, hbm, hbm],
-        out_specs=(vmem, hbm),
+        out_specs=(hbm, hbm),
         scratch_shapes=scratch,
         compiler_params=pltpu.CompilerParams(
             collective_id=0, has_side_effects=True, vmem_limit_bytes=63 * 1024 * 1024

time: 65.6 us -> 64.3 us (0.980)
  Pallas kernels: 59.4 us -> 58.3 us
    pallas_call x1, Pallas kernels: 59.4 us -> 58.3 us  [body(): call(pair, length, ln_gain.reshape(1, 128), w_query, w_key, w_value, w_ga...]
where the time goes in v7:
time: 64.3 us; the launch traced here: 63.3 us
  Pallas kernels  58.3 us (91%)
  local copies, waits for them, and re-layouts  3.74 us (6%)
  between operations  1.29 us (2%)
    pallas_call x1, Pallas kernels, body(): call(pair, length, ln_gain.reshape(1, 128), w_query, w_key, w_value, w_ga...  58.3 us
    unnamed x2, local copies, waits for them, and re-layouts  3.74 us

profile of v7, /device:TPU:1, one launch (start us, length us, event | category | flops | bytes accessed | tf_op | source)
XLA Modules:
  0.0 63.3 jit_solution(17134568086988710268)
XLA Ops:
  1.3 58.3 %shard_map.113 = (bf16[8,32,128]{2,1,0:T(8,128)(2,1)}, f32[4,16,32,128]{3,2,1,0:T(8,128)}) custom-call(bf16[64,32,128]{2,1,0:T(8,128)(2,1)} %pair_h.1, s32[1]{0:T(128)S(6)} %copy.14.length, f32[1,128]{1,0:T(1,128)} %bitcast.5, bf16[128,128]{1,0:T(8,128)(2,1)} %w_query_h.1, bf16[128,128]{1,0:T(8,128)(2,1)} %w_key_h.1, bf16[128,128]{1,0:T(8,128)(2,1)} %w_value_h.1, ...), custom_call_target="tpu_custom_call" | custom-call | tf_op jit(solution)/shard_map/pallas_call | solution.py:501
  59.6 1.5 %copy.15 = bf16[8,32,128]{2,1,0:T(8,128)(2,1)} copy(bf16[8,32,128]{2,1,0:T(8,128)(2,1)} %get-tuple-element.8) | data formatting | bytes 131072
  61.1 2.3 %copy.16 = f32[64,32,128]{2,1,0:T(8,128)} copy(f32[64,32,128]{2,1,0:T(8,128)} %bitcast.3) | data formatting | bytes 2097152

commit v8 on v7

--- a/solution.py
+++ b/solution.py
@@ -434,6 +434,19 @@
     def _():
         for copy in turned:
             copy.wait_send()
+
+
+def hand_over(update, pair_grad, update_out, pair_grad_out, sems):
+    copies = [pltpu.make_async_copy(update, update_out, sems.at[8])]
+    for q in range(4):
+        for n in range(2):
+            part = pl.ds(n * 8, 8)
+            copies.append(pltpu.make_async_copy(
+                pair_grad.at[q, part], pair_grad_out.at[q, part], sems.at[q * 2 + n]))
+    for copy in copies:
+        copy.start()
+    for copy in copies:
+        copy.wait()
 
 
 def body(pair, length, ln_gain, w_query, w_key, w_value, w_gate, w_bias, w_out, out_grad):
@@ -502,6 +515,17 @@
         pair, length, ln_gain.reshape(1, 128), w_query, w_key, w_value, w_gate, w_bias.T, w_out,
         out_grad,
     )
+    update, pair_grad = pl.pallas_call(
+        hand_over,
+        out_shape=(
+            jax.ShapeDtypeStruct(update.shape, bf16),
+            jax.ShapeDtypeStruct(pair_grad.shape, f32),
+        ),
+        in_specs=[hbm, hbm],
+        out_specs=(hbm, hbm),
+        scratch_shapes=[pltpu.SemaphoreType.DMA((9,))],
+        compiler_params=pltpu.CompilerParams(vmem_limit_bytes=63 * 1024 * 1024),
+    )(update, pair_grad)
     return update, pair_grad.reshape(pair.shape)
 
 

time: 64.3 us -> 95.4 us (1.48)
  Pallas kernels: 58.3 us -> 93.2 us
  local copies, waits for them, and re-layouts: 3.74 us -> 0 us
    pallas_call x0 -> x1, Pallas kernels: none -> 34.9 us  [body(): pl.pallas_call(hand_over, out_shape=(jax.ShapeDtypeStruct(update.shape, b...]
    unnamed x2 -> x0, local copies, waits for them, and re-layouts: 3.74 us -> none
where the time goes in v8:
time: 95.4 us; the launch traced here: 94.5 us
  Pallas kernels  93.2 us (98%)
  between operations  1.29 us (1%)
    pallas_call x1, Pallas kernels, body(): call(pair, length, ln_gain.reshape(1, 128), w_query, w_key, w_value, w_ga...  58.3 us
    pallas_call x1, Pallas kernels, body(): pl.pallas_call(hand_over, out_shape=(jax.ShapeDtypeStruct(update.shape, b...  34.9 us

profile of v8, /device:TPU:1, one launch (start us, length us, event | category | flops | bytes accessed | tf_op | source)
XLA Modules:
  0.0 94.5 jit_solution(6325971330091228871)
XLA Ops:
  1.3 58.3 %shard_map.113 = (bf16[8,32,128]{2,1,0:T(8,128)(2,1)}, f32[4,16,32,128]{3,2,1,0:T(8,128)}) custom-call(bf16[64,32,128]{2,1,0:T(8,128)(2,1)} %pair_h.1, s32[1]{0:T(128)S(6)} %copy.12.length, f32[1,128]{1,0:T(1,128)} %bitcast.4, bf16[128,128]{1,0:T(8,128)(2,1)} %w_query_h.1, bf16[128,128]{1,0:T(8,128)(2,1)} %w_key_h.1, bf16[128,128]{1,0:T(8,128)(2,1)} %w_value_h.1, ...), custom_call_target="tpu_custom_call" | custom-call | tf_op jit(solution)/shard_map/pallas_call | solution.py:514
  59.5 34.9 %shard_map.114 = (bf16[8,32,128]{2,1,0:T(8,128)(2,1)}, f32[4,16,32,128]{3,2,1,0:T(8,128)}) custom-call(bf16[8,32,128]{2,1,0:T(8,128)(2,1)} %get-tuple-element.6.update, f32[4,16,32,128]{3,2,1,0:T(8,128)} %get-tuple-element.7.pair_grad), custom_call_target="tpu_custom_call" | custom-call | tf_op jit(solution)/shard_map/pallas_call | solution.py:518
